TPU v7x, 256 devices: a whole 4x4x8 slice. The times are simulated.
256 devices in a mesh: ctx: 64 (over z, x, core), head: 4 (over y).
Axes of the slice: x: 4, y: 4, z: 8, core: 2. Of those that a mesh axis runs over, the one named last changes fastest.
Arguments:
- q_pre: bfloat16 [16384, 2560], P('ctx', 'head'), may hold values from -48 to 48
- k_pre: bfloat16 [16384, 2560], P('ctx', 'head'), may hold values from -48 to 48
- values: bfloat16 [16384, 2560], P('ctx', 'head'), may hold values from -6 to 6
- out_grad: bfloat16 [16384, 2560], P('ctx', 'head'), may hold values from -192 to 192
- q_gain: float32 [2560], P('head'), may hold values from 0.25 to 1.75
- k_gain: float32 [2560], P('head'), may hold values from 0.25 to 1.75
- selected: int32 [128, 20, 7], P('ctx', 'head'), may hold values from 0 to 127, as said below
Outputs:
- dq_pre: bfloat16 [16384, 2560], P('ctx', 'head')
- dk_pre: bfloat16 [16384, 2560], P('ctx', 'head')
- dv: bfloat16 [16384, 2560], P('ctx', 'head')
Inputs may be any that keep to these rules, and one draw needn't show every extreme that they name: `selected`: entry [i, h, c] names a tile outside the block of query tile i; the 7 entries of one row lie in 7 different blocks. All query tiles of one block have equal rows for each head. Over the heads of one group of 5 consecutive heads starting at a multiple of 5, the rows of one block name no other block more than 1 times in all, and some block exactly 1 times.
All inputs are finite; a program needn't handle non-finite values.
Results may differ from a plain program's by a relative error of at most 0.011.
Values may be sent and summed in bfloat16 or wider, within the bound.
A program may use at most 128 MiB of HBM per device.

v0:
```python
import math

import jax
import jax.numpy as jnp
from jax import lax
from jax.sharding import PartitionSpec as P

HD = 128
TILE = 128


epsilon = 1e-06


def split_heads(array, heads_dev):
    return array.reshape(array.shape[0], heads_dev, HD).transpose(1, 0, 2)


def merge_heads(array):
    heads_dev, tok_dev, depth = array.shape
    return array.transpose(1, 0, 2).reshape(tok_dev, heads_dev * depth)


def per_tile(array, qt_dev):
    heads_dev, tok_dev, depth = array.shape
    return array.reshape(heads_dev, qt_dev, TILE, depth).transpose(1, 0, 2, 3)


def from_tiles(array):
    qt_dev, heads_dev, rows_tile, depth = array.shape
    return array.transpose(1, 0, 2, 3).reshape(heads_dev, qt_dev * rows_tile, depth)


def table_sum(taken, pieces, heads_dev, qt_dev):
    flat_pieces = pieces.reshape(pieces.shape[0], -1)
    summed = jnp.dot(
        taken, flat_pieces, precision=lax.Precision.HIGHEST, preferred_element_type=jnp.float32
    )
    summed = summed.reshape(heads_dev, qt_dev, 2, TILE, HD).transpose(2, 0, 1, 3, 4)
    return summed.reshape(2, heads_dev, qt_dev * TILE, HD)


def rounded(array):
    return array.astype(jnp.bfloat16)


def finish_norm(wide, scale, gain, grad, dot_sum, width_all):
    return (scale * gain * grad - wide * scale**3 * (dot_sum / width_all)[:, None]).astype(
        jnp.bfloat16
    )


def on_device(q_pre, k_pre, values, out_grad, q_gain, k_gain, selected):
    n_ctx = lax.axis_size("ctx")
    tok_dev, width_dev = q_pre.shape
    width_all = width_dev * lax.axis_size("head")
    heads_dev = width_dev // HD
    qt_dev = tok_dev // TILE
    remote_count = selected.shape[2]
    factor = 1.0 / math.sqrt(HD)
    q_wide = q_pre.astype(jnp.float32)
    k_wide = k_pre.astype(jnp.float32)
    q_square, k_square = lax.psum(
        (jnp.sum(q_wide * q_wide, axis=1), jnp.sum(k_wide * k_wide, axis=1)), "head"
    )
    q_scale = lax.rsqrt(q_square / width_all + epsilon)[:, None]
    k_scale = lax.rsqrt(k_square / width_all + epsilon)[:, None]
    q_heads = split_heads(rounded(q_wide * q_scale * q_gain), heads_dev)
    k_heads = split_heads(rounded(k_wide * k_scale * k_gain), heads_dev)
    v_heads = split_heads(values, heads_dev)
    g_heads = split_heads(out_grad, heads_dev)
    q_tiles = per_tile(q_heads, qt_dev)
    g_tiles = per_tile(g_heads, qt_dev)
    k_table = k_heads.reshape(heads_dev * qt_dev, TILE, HD)
    v_table = v_heads.reshape(heads_dev * qt_dev, TILE, HD)
    flat_sel = selected[0].reshape(-1)
    n_slot = flat_sel.shape[0]
    capacity = -(-n_slot // (n_ctx - 1))
    n_buffer = n_ctx * capacity
    owners = flat_sel // qt_dev
    head_of = jnp.arange(n_slot, dtype=jnp.int32) // remote_count
    codes = head_of * qt_dev + flat_sel % qt_dev
    matches = (owners[:, None] == jnp.arange(n_ctx, dtype=jnp.int32)[None, :]).astype(jnp.int32)
    ranks = jnp.sum((jnp.cumsum(matches, axis=0) - matches) * matches, axis=1)
    position = owners * capacity + ranks
    placed = position[None, :] == jnp.arange(n_buffer, dtype=jnp.int32)[:, None]
    request = jnp.sum(jnp.where(placed, codes[None, :] + 1, 0), axis=1) - 1
    asked = lax.all_to_all(
        request.reshape(n_ctx, capacity), "ctx", split_axis=0, concat_axis=0, tiled=True
    ).reshape(n_buffer)
    clipped = jnp.maximum(asked, 0)
    taken = (asked[None, :] == jnp.arange(heads_dev * qt_dev, dtype=jnp.int32)[:, None]).astype(
        jnp.float32
    )
    s_near = (
        jnp.einsum("rhqd,hkd->rhqk", q_tiles, k_heads, preferred_element_type=jnp.float32) * factor
    )
    dp_near = jnp.einsum("rhqd,hkd->rhqk", g_tiles, v_heads, preferred_element_type=jnp.float32)
    near_top = jnp.max(s_near, axis=-1)
    outgoing = jnp.stack((k_table[clipped], v_table[clipped]), axis=1).reshape(
        n_ctx, capacity, 2, TILE, HD
    )
    incoming = lax.all_to_all(outgoing, "ctx", split_axis=0, concat_axis=0, tiled=True).reshape(
        n_buffer, 2, TILE, HD
    )
    slot_kv = incoming[position].reshape(heads_dev, remote_count, 2, TILE, HD)
    far_k = slot_kv[:, :, 0]
    far_v = slot_kv[:, :, 1]
    s_far = (
        jnp.einsum("rhqd,hckd->rhqck", q_tiles, far_k, preferred_element_type=jnp.float32) * factor
    )
    dp_far = jnp.einsum("rhqd,hckd->rhqck", g_tiles, far_v, preferred_element_type=jnp.float32)
    row_top = jnp.maximum(near_top, jnp.max(s_far, axis=(-2, -1)))
    totals = jnp.sum(jnp.exp(s_near - row_top[..., None]), axis=-1) + jnp.sum(
        jnp.exp(s_far - row_top[..., None, None]), axis=(-2, -1)
    )
    lse = row_top + jnp.log(totals)
    p_near = jnp.exp(s_near - lse[..., None])
    p_far = jnp.exp(s_far - lse[..., None, None])
    delta = jnp.sum(p_near * dp_near, axis=-1) + jnp.sum(p_far * dp_far, axis=(-2, -1))
    ds_near = rounded(p_near * (dp_near - delta[..., None]) * factor)
    pb_near = rounded(p_near)
    dq_near = jnp.einsum("rhqk,hkd->rhqd", ds_near, k_heads, preferred_element_type=jnp.float32)
    dk_near = jnp.einsum("rhqk,rhqd->hkd", ds_near, q_tiles, preferred_element_type=jnp.float32)
    dv_near = jnp.einsum("rhqk,rhqd->hkd", pb_near, g_tiles, preferred_element_type=jnp.float32)
    dq_near, dk_near, dv_near = (dq_near, dk_near, dv_near)
    ds_far = rounded(p_far * (dp_far - delta[..., None, None]) * factor)
    pb_far = rounded(p_far)
    dq_far = jnp.einsum("rhqck,hckd->rhqd", ds_far, far_k, preferred_element_type=jnp.float32)
    dq_wide = merge_heads(from_tiles(dq_near + dq_far))
    q_dot = jnp.sum(q_gain * dq_wide * q_wide, axis=1)
    dq_wide, q_dot = (dq_wide, q_dot)
    dk_far = jnp.einsum("rhqck,rhqd->hckd", ds_far, q_tiles, preferred_element_type=jnp.float32)
    dv_far = jnp.einsum("rhqck,rhqd->hckd", pb_far, g_tiles, preferred_element_type=jnp.float32)
    grads = jnp.stack((dk_far, dv_far), axis=2).reshape(n_slot, 2, TILE, HD)
    sending = jnp.zeros((n_buffer, 2, TILE, HD), jnp.float32).at[position].set(grads)
    returned = lax.all_to_all(
        sending.reshape(n_ctx, capacity, 2, TILE, HD),
        "ctx",
        split_axis=0,
        concat_axis=0,
        tiled=True,
    ).reshape(n_buffer, 2, TILE, HD)
    far_sums = table_sum(taken, returned, heads_dev, qt_dev)
    dk_wide = merge_heads(dk_near + far_sums[0])
    dv_heads = dv_near + far_sums[1]
    k_dot = jnp.sum(k_gain * dk_wide * k_wide, axis=1)
    q_dot, k_dot = lax.psum((q_dot, k_dot), "head")
    dq_result = finish_norm(q_wide, q_scale, q_gain, dq_wide, q_dot, width_all)
    dk_result = finish_norm(k_wide, k_scale, k_gain, dk_wide, k_dot, width_all)
    return (dq_result, dk_result, merge_heads(dv_heads).astype(jnp.bfloat16))


def solution(mesh):
    placed = (
        P("ctx", "head"),
        P("ctx", "head"),
        P("ctx", "head"),
        P("ctx", "head"),
        P("head"),
        P("head"),
        P("ctx", "head", None),
    )
    return jax.shard_map(
        on_device,
        mesh=mesh,
        in_specs=placed,
        out_specs=(P("ctx", "head"), P("ctx", "head"), P("ctx", "head")),
        check_vma=False,
    )
```

profile of v0, /device:TPU:1, one launch (start us, length us, event | category | flops | bytes accessed | tf_op | source)
XLA Modules:
  0.0 404.9 jit_solution(9981801172890778202)
XLA Ops:
  2.6 13.0 %all-to-all-start = ((s32[64,1,1]{2,1,0:T(1,128)}), s32[64,1,1]{2,1,0:T(1,128)S(1)}, u32[]{:S(2)}, u32[]{:S(2)}) async-start(s32[64,1,1]{2,1,0:T(1,128)} %copy.144), calls=%async_computation | async-start | bytes 65536 | tf_op jit(solution)/shard_map/all_to_all | solution.py:88
  15.6 1.1 copy.139
  16.8 1.1 copy.140
  18.2 9.0 %all-reduce.1 = (f32[256]{0:T(256)S(1)}, f32[256]{0:T(256)S(1)}) all-reduce(f32[256]{0:T(256)S(1)} %fusion.33, f32[256]{0:T(256)S(1)} %fusion.26), channel_id=1, replica_groups=mesh['ctx'=64,'head'=4] {'head'}, use_global_device_ids=true, to_apply=%region_3.0 | all-reduce | flops 512 | bytes 4096 | tf_op jit(solution)/shard_map/psum | solution.py:63
  29.2 2.4 fusion.51
  32.5 2.2 gather_fusion
  34.7 2.0 maximum_bitcast_fusion
  36.7 2.3 copy.147
  39.0 12.4 %all-to-all-start.1 = ((bf16[64,1,2,128,128]{4,3,2,1,0:T(8,128)(2,1)}), bf16[64,1,2,128,128]{4,3,2,1,0:T(8,128)(2,1)}, u32[]{:S(2)}, u32[]{:S(2)}) async-start(bf16[64,1,2,128,128]{4,3,2,1,0:T(8,128)(2,1)} %copy.147), calls=%async_computation.1 | async-start | bytes 8388608 | tf_op jit(solution)/shard_map/all_to_all | solution.py:103
  52.7 93.0 %all-to-all-done.1 = bf16[64,1,2,128,128]{4,3,2,1,0:T(8,128)(2,1)} async-done(((bf16[64,1,2,128,128]{4,3,2,1,0:T(8,128)(2,1)}), bf16[64,1,2,128,128]{4,3,2,1,0:T(8,128)(2,1)}, u32[]{:S(2)}, u32[]{:S(2)}) %all-to-all-start.1) | async-done | bytes 4194336 | tf_op jit(solution)/shard_map/all_to_all | solution.py:103
  145.7 4.6 %gather_fusion.2 = bf16[35,2,128,128]{3,2,1,0:T(8,128)(2,1)} fusion(bf16[64,2,128,128]{3,2,1,0:T(8,128)(2,1)} %bitcast.17, s32[1024]{0:T(1024)S(1)} %pad_clamp_fusion), kind=kCustom, calls=%fused_computation.2 | custom fusion | bytes 4587660 | tf_op jit(solution)/shard_map/gather | solution.py:106
  150.3 1.8 copy.148
  153.9 1.1 fusion.3
  156.0 1.5 multiply_reduce_fusion
  157.5 1.3 fusion.6
  160.2 2.5 pad_maximum_fusion
  162.7 4.3 %broadcast_in_dim.12 = f32[64,2,128,128]{3,2,1,0:T(8,128)} broadcast(f32[]{:T(128)} %constant.53.clone.1), dimensions={} | broadcast | bytes 8388612 | tf_op jit(solution)/shard_map/broadcast_in_dim | solution.py:136
  167.0 11.0 %scatter_fusion = f32[64,2,128,128]{3,2,1,0:T(8,128)} fusion(f32[64,2,128,128]{3,2,1,0:T(8,128)} %broadcast_in_dim.12, s32[35]{0:T(128)S(1)} %fusion.49, f32[35,2,128,128]{3,2,1,0:T(8,128)} %pad_maximum_fusion), kind=kCustom, calls=%fused_computation.3 | custom fusion | bytes 13762700 | tf_op jit(solution)/shard_map/scatter | solution.py:136
  177.9 7.7 %all-to-all-start.2 = ((f32[64,1,2,128,128]{4,3,2,1,0:T(8,128)}), f32[64,1,2,128,128]{4,3,2,1,0:T(8,128)}, u32[]{:S(2)}, u32[]{:S(2)}) async-start(f32[64,1,2,128,128]{4,3,2,1,0:T(8,128)} %bitcast.200), calls=%async_computation.2 | async-start | bytes 16777216 | tf_op jit(solution)/shard_map/all_to_all | solution.py:137
  185.7 3.0 convolution_bitcast_fusion.1
  189.7 1.2 convolution_add_fusion
  190.9 1.3 copy.155
  192.4 176.0 %all-to-all-done.2 = f32[64,1,2,128,128]{4,3,2,1,0:T(8,128)} async-done(((f32[64,1,2,128,128]{4,3,2,1,0:T(8,128)}), f32[64,1,2,128,128]{4,3,2,1,0:T(8,128)}, u32[]{:S(2)}, u32[]{:S(2)}) %all-to-all-start.2) | async-done | bytes 8388640 | tf_op jit(solution)/shard_map/all_to_all | solution.py:137
  368.4 8.1 %copy.207 = f32[8,8,256,128]{3,1,2,0:T(8,128)S(1)} copy(f32[8,8,256,128]{3,2,1,0:T(8,128)} %bitcast.103) | data formatting | bytes 16777216
  376.5 1.5 copy.199
  378.0 8.4 %fusion.15 = f32[2,5,2,128,128]{4,1,3,0,2:T(8,128)S(1)} fusion(f32[2,128,128,64]{2,1,0,3:T(8,128)S(1)} %bitcast.201, s32[5,2]{0,1:T(2,128)S(1)} %multiply_add_fusion, s32[64]{0:T(128)S(1)} %get-tuple-element.21), kind=kOutput, calls=%fused_computation.26 | convolution fusion | flops 251658880 | bytes 9699624 | tf_op jit(solution)/shard_map/dot_general | solution.py:36
  386.4 1.5 fusion.52
  387.9 2.3 copy.197
  390.2 1.7 fusion.19
  392.9 6.0 %all-reduce = (f32[256]{0:T(256)S(1)}, f32[256]{0:T(256)S(1)}) all-reduce(f32[256]{0:T(256)S(1)} %fusion.32, f32[256]{0:T(256)S(1)} %fusion.39), channel_id=1, replica_groups=mesh['ctx'=64,'head'=4] {'head'}, use_global_device_ids=true, to_apply=%region_14.15 | all-reduce | flops 512 | bytes 4096 | tf_op jit(solution)/shard_map/psum | solution.py:148
  399.9 1.2 fusion.38
  402.1 1.5 copy.165
  (75 shorter events, 16.0 us)
Async XLA Ops:
  0.6 27.4 %copy-start.10 = (bf16[256,640]{1,0:T(8,128)(2,1)S(1)}, bf16[256,640]{1,0:T(8,128)(2,1)}, u32[]{:S(2)}) copy-start(bf16[256,640]{1,0:T(8,128)(2,1)} %param.9) | copy-start | bytes 983044
  2.6 26.5 %all-to-all-start = ((s32[64,1,1]{2,1,0:T(1,128)}), s32[64,1,1]{2,1,0:T(1,128)S(1)}, u32[]{:S(2)}, u32[]{:S(2)}) async-start(s32[64,1,1]{2,1,0:T(1,128)} %copy.144), calls=%async_computation | async-start | bytes 65536 | tf_op jit(solution)/shard_map/all_to_all | solution.py:88
  28.0 3.5 copy-start.4
  28.2 0.7 copy-start.8
  39.0 12.5 %copy-start.12 = (f32[640]{0:T(1024)S(1)}, f32[640]{0:T(1024)}, u32[]{:S(2)}) copy-start(f32[640]{0:T(1024)} %param.11) | copy-start | bytes 7684
  39.0 12.8 %copy-start.11 = (bf16[256,640]{1,0:T(8,128)(2,1)S(1)}, bf16[256,640]{1,0:T(8,128)(2,1)}, u32[]{:S(2)}) copy-start(bf16[256,640]{1,0:T(8,128)(2,1)} %param.10) | copy-start | bytes 983044
  39.0 106.8 %all-to-all-start.1 = ((bf16[64,1,2,128,128]{4,3,2,1,0:T(8,128)(2,1)}), bf16[64,1,2,128,128]{4,3,2,1,0:T(8,128)(2,1)}, u32[]{:S(2)}, u32[]{:S(2)}) async-start(bf16[64,1,2,128,128]{4,3,2,1,0:T(8,128)(2,1)} %copy.147), calls=%async_computation.1 | async-start | bytes 8388608 | tf_op jit(solution)/shard_map/all_to_all | solution.py:103
  51.3 1.0 copy-start.5
  152.1 1.8 copy-start
  155.0 1.0 copy-start.9
  158.8 1.4 copy-start.1
  177.9 190.4 %all-to-all-start.2 = ((f32[64,1,2,128,128]{4,3,2,1,0:T(8,128)}), f32[64,1,2,128,128]{4,3,2,1,0:T(8,128)}, u32[]{:S(2)}, u32[]{:S(2)}) async-start(f32[64,1,2,128,128]{4,3,2,1,0:T(8,128)} %bitcast.200), calls=%async_computation.2 | async-start | bytes 16777216 | tf_op jit(solution)/shard_map/all_to_all | solution.py:137
  185.7 3.0 copy-start.7
  188.7 1.0 copy-start.6
  189.7 1.2 copy-start.3
  387.9 4.8 %copy-start.13 = (f32[640]{0:T(1024)S(1)}, f32[640]{0:T(1024)}, u32[]{:S(2)}) copy-start(f32[640]{0:T(1024)} %param.12) | copy-start | bytes 7684
  391.8 0.9 copy-start.2
where the time goes:
time: 411 us; the launch traced here: 405 us
  waiting for transfers between devices  269 us (65%)
  local copies, waits for them, and re-layouts  53.8 us (13%)
  starting transfers between devices  33.1 us (8%)
  matrix products  20 us (5%)
  blocking collectives  15 us (4%)
  other arithmetic  13 us (3%)
    all_to_all x1, waiting for transfers between devices, on_device(): lax.all_to_all(sending.reshape(n_ctx, capacity, 2, TILE, HD), 'ctx', spli...  176 us
    all_to_all x1, waiting for transfers between devices, on_device(): lax.all_to_all(outgoing, 'ctx', split_axis=0, concat_axis=0, tiled=True)  93 us
    unnamed x37, local copies, waits for them, and re-layouts  17.7 us
    all_to_all x1, starting transfers between devices, on_device(): lax.all_to_all(request.reshape(n_ctx, capacity), 'ctx', split_axis=0, con...  13 us
    all_to_all x1, starting transfers between devices, on_device(): lax.all_to_all(outgoing, 'ctx', split_axis=0, concat_axis=0, tiled=True)  12.4 us
    scatter x1, local copies, waits for them, and re-layouts, on_device(): jnp.zeros((n_buffer, 2, TILE, HD), jnp.float32).at[position].set(grads)  11 us
    psum x1, blocking collectives, on_device(): lax.psum((jnp.sum(q_wide * q_wide, axis=1), jnp.sum(k_wide * k_wide, axis...  9.02 us
    dot_general x1, matrix products, table_sum(): jnp.dot(taken, flat_pieces, precision=lax.Precision.HIGHEST, preferred_el...  8.4 us
  transfers between devices with their start and end apart: 3, of which 2 were waited for; matrix products, arithmetic and copies ran while one was open for 3% of the time, Pallas kernels for 0%

commit v1 on v0

v1 whole, which is shorter than its diff:
```python
import functools
import math

import jax
import jax.numpy as jnp
from jax import lax
from jax.experimental import pallas as pl
from jax.experimental.pallas import tpu as pltpu
from jax.sharding import PartitionSpec as P

HD = 128
TILE = 128
NH = 5
REM = 7
NT = 2 * NH
NZ = 8
NP = 8
NY = 4
TOK = 2 * TILE
EPS = 1e-6
FACTOR = 1.0 / math.sqrt(HD)
MESH = pl.DeviceIdType.MESH
F32 = jnp.float32
BF16 = jnp.bfloat16


def dot_nt(a, b):
    return lax.dot_general(a, b, (((1,), (1,)), ((), ())), preferred_element_type=F32)


def dot_nn(a, b):
    return lax.dot_general(a, b, (((1,), (0,)), ((), ())), preferred_element_type=F32)


def dot_tn(a, b):
    return lax.dot_general(a, b, (((0,), (0,)), ((), ())), preferred_element_type=F32)


def fold_rows(array, op):
    parts = [array[8 * i : 8 * i + 8] for i in range(array.shape[0] // 8)]
    while len(parts) > 1:
        parts = [op(parts[i], parts[i + 1]) for i in range(0, len(parts), 2)]
    return parts[0]


def kernel(width_all, *refs):
    sel, q_in, k_in, v_in, g_in, q_gain, k_gain, dq_out, dk_out, dv_out = refs[:10]
    scratch = list(refs[10:])
    v_bufs = [scratch.pop(0) for _ in range(NZ)]
    k_bufs = [scratch.pop(0) for _ in range(NZ)]
    bufs = (v_bufs, k_bufs)
    (
        staged,
        v_got,
        k_got,
        s_all,
        dp_all,
        ds_all,
        back_x,
        back_z,
        s_near,
        dp_near,
        q_heads,
        g_heads,
        lse_ref,
        delta_ref,
        dq_wide,
        dk_sum,
        dv_sum,
        q_scale_ref,
        k_scale_ref,
        y_out,
        y_in,
        req_v,
        req_s,
        zf_send,
        zf_recv,
        xf_send,
        xf_recv,
        xb_send,
        xb_recv,
        zb_send,
        zb_recv,
        y_send,
        y_recv,
        rq_send,
        rq_recv,
        here_sem,
    ) = scratch
    got = (v_got, k_got)

    me = lax.axis_index("ctx")
    group = lax.axis_index("head")
    z = me // NP
    xc = lax.rem(me, NP)

    def in_plane(p):
        return {"ctx": z * NP + lax.rem(xc + p, NP), "head": group}

    z_next = (
        {"ctx": lax.rem(z + 1, NZ) * NP + xc, "head": group},
        {"ctx": lax.rem(z + NZ - 1, NZ) * NP + xc, "head": group},
    )

    def along_y(p):
        return {"ctx": me, "head": lax.rem(group + p, NY)}

    barrier = pltpu.get_barrier_semaphore()
    for p in range(1, NP):
        pl.semaphore_signal(barrier, inc=1, device_id=in_plane(p), device_id_type=MESH)
    for d in range(2):
        pl.semaphore_signal(barrier, inc=1, device_id=z_next[d], device_id_type=MESH)
    for p in range(1, NY):
        pl.semaphore_signal(barrier, inc=1, device_id=along_y(p), device_id_type=MESH)

    for t in range(2):
        for h in range(NH):
            rows, cols = slice(t * TILE, (t + 1) * TILE), slice(h * HD, (h + 1) * HD)
            v_bufs[0][t * NH + h] = v_in[rows, cols]
    lane = lax.broadcasted_iota(jnp.int32, (8, 128), 1)
    wanted = jnp.full((8, 128), -1, jnp.int32)
    for h in range(NH):
        for c in range(REM):
            tile = sel[0, h, c]
            wanted = jnp.where(lane == (tile >> 1), (tile & 1) * NH + h, wanted)
    req_v[xc] = wanted

    def squares(ref):
        wide = ref[...].astype(F32)
        return jnp.sum(wide * wide, axis=1, keepdims=True)

    lanes_tok = lax.broadcasted_iota(jnp.int32, (TOK, 128), 1)

    def as_rows(first, second):
        both = jnp.where(lanes_tok == 0, first, jnp.where(lanes_tok == 1, second, 0.0))
        return jnp.transpose(both)[:8]

    def as_columns(rows):
        tall = jnp.transpose(jnp.concatenate([rows, jnp.zeros((120, TOK), F32)], axis=0))
        return tall[:, 0:1], tall[:, 1:2]

    def y_copy(n, p):
        return pltpu.make_async_remote_copy(
            src_ref=y_out.at[n],
            dst_ref=y_in.at[n, p - 1],
            send_sem=y_send.at[n, p - 1],
            recv_sem=y_recv.at[n, p - 1],
            device_id=along_y(p),
            device_id_type=MESH,
        )

    def y_start(n, first, second):
        y_out[n] = as_rows(first, second)
        for p in range(1, NY):
            y_copy(n, p).start()

    def y_total(n):
        for p in range(1, NY):
            y_copy(n, p).wait_recv()
        return (y_out[n] + y_in[n, 0]) + (y_in[n, 1] + y_in[n, 2])

    q_square, k_square = squares(q_in), squares(k_in)
    pl.semaphore_wait(barrier, NP - 1 + 2 + NY - 1)

    def req_copy(p):
        return pltpu.make_async_remote_copy(
            src_ref=req_v.at[xc],
            dst_ref=req_v.at[xc],
            send_sem=rq_send.at[p - 1],
            recv_sem=rq_recv.at[p - 1],
            device_id=in_plane(p),
            device_id_type=MESH,
        )

    def zf_copy(d, hop, kind, t):
        source = (NZ + 1 - hop) % NZ if d == 0 else hop - 1
        target = NZ - hop if d == 0 else hop
        at = ((hop - 1) * 2 + kind) * 2 + t
        part = pl.ds(t * NH, NH)
        return pltpu.make_async_remote_copy(
            src_ref=bufs[kind][source].at[part],
            dst_ref=bufs[kind][target].at[part],
            send_sem=zf_send.at[d, at],
            recv_sem=zf_recv.at[d, at],
            device_id=z_next[d],
            device_id_type=MESH,
        )

    y_start(0, q_square, k_square)
    for p in range(1, NP):
        req_copy(p).start()
    for t in range(2):
        for d in range(2):
            zf_copy(d, 1, 0, t).start()

    total = y_total(0)
    q_scale, k_scale = as_columns(lax.rsqrt(total / width_all + EPS))
    q_scale_ref[...] = jnp.broadcast_to(q_scale, (TOK, 128))
    k_scale_ref[...] = jnp.broadcast_to(k_scale, (TOK, 128))
    for t in range(2):
        for h in range(NH):
            rows, cols = slice(t * TILE, (t + 1) * TILE), slice(h * HD, (h + 1) * HD)
            k_bufs[0][t * NH + h] = (
                k_in[rows, cols].astype(F32) * k_scale_ref[rows] * k_gain[:, cols]
            ).astype(BF16)
        for d in range(2):
            zf_copy(d, 1, 1, t).start()

    for p in range(1, NP):
        req_copy(p).wait_recv()
    table = pltpu.make_async_copy(req_v, req_s, here_sem.at[0])
    table.start()
    for h in range(NH):
        cols = slice(h * HD, (h + 1) * HD)
        q_heads[h] = (
            q_in[:, cols].astype(F32) * q_scale_ref[...] * q_gain[:, cols]
        ).astype(BF16)
        g_heads[h] = g_in[:, cols]
    table.wait()

    def plane_of(r):
        return lax.rem(z + r, NZ)

    def xf_copy(kind, r, p):
        return pltpu.make_async_remote_copy(
            src_ref=staged.at[(kind * NZ + r) * NP + p],
            dst_ref=got[kind].at[plane_of(r) * NP + xc],
            send_sem=xf_send.at[kind * NZ + r],
            recv_sem=xf_recv.at[kind * NZ + r],
            device_id=in_plane(p),
            device_id_type=MESH,
        )

    def spread(kind, r):
        slot = plane_of(r) * NP + xc
        source = bufs[kind][r]

        def one(p, carry):
            code = jnp.maximum(req_s[lax.rem(xc + p, NP), 0, slot], 0)
            staged[(kind * NZ + r) * NP + p] = source[code]
            xf_copy(kind, r, p).start()
            return carry

        lax.fori_loop(1, NP, one, 0)
        got[kind][slot] = source[jnp.maximum(req_s[xc, 0, slot], 0)]

    def xf_all(kind, r):
        first = (kind * NZ + r) * NP + 1
        return pltpu.make_async_remote_copy(
            src_ref=staged.at[pl.ds(first, NP - 1)],
            dst_ref=got[kind].at[pl.ds(0, NP - 1)],
            send_sem=xf_send.at[kind * NZ + r],
            recv_sem=xf_recv.at[kind * NZ + r],
            device_id=in_plane(1),
            device_id_type=MESH,
        )

    def scores(r):
        for kind in range(2):
            xf_all(kind, r).wait_recv()

        def one(j, carry):
            slot = plane_of(r) * NP + j
            head = lax.rem(jnp.maximum(req_s[xc, 0, slot], 0), NH)
            s_all[slot] = dot_nt(k_got[slot], q_heads[head]) * FACTOR
            dp_all[slot] = dot_nt(v_got[slot], g_heads[head])
            return carry

        lax.fori_loop(0, NP, one, 0)

    def near_scores():
        def one(h, carry):
            for t in range(2):
                s_near[h, t] = dot_nt(k_bufs[0][t * NH + h], q_heads[h]) * FACTOR
                dp_near[h, t] = dot_nt(v_bufs[0][t * NH + h], g_heads[h])
            return carry

        lax.fori_loop(0, NH, one, 0)

    spread(0, 0)
    spread(1, 0)
    near_scores()
    for hop in range(1, 4):
        for kind in range(2):
            for t in range(2):
                for d in range(2):
                    zf_copy(d, hop, kind, t).wait_recv()
                    if hop < 3 or t == d:
                        zf_copy(d, hop + 1, kind, t).start()
            spread(kind, NZ - hop)
            spread(kind, hop)
        if hop == 1:
            scores(0)
        else:
            scores(NZ - hop + 1)
            scores(hop - 1)
    for kind in range(2):
        zf_copy(0, 4, kind, 0).wait_recv()
        zf_copy(1, 4, kind, 1).wait_recv()
        spread(kind, 4)
    scores(5)
    scores(3)
    scores(4)

    for p in range(1, NP):
        req_copy(p).wait_send()
    for hop in range(1, 5):
        for kind in range(2):
            for t in range(2):
                for d in range(2):
                    if hop < 4 or t == d:
                        zf_copy(d, hop, kind, t).wait_send()
    for kind in range(2):
        for r in range(NZ):
            xf_all(kind, r).wait_send()

    def stats(h, carry):
        places = [sel[0, h, c] >> 1 for c in range(REM)]
        top = jnp.maximum(
            fold_rows(s_near[h, 0], jnp.maximum), fold_rows(s_near[h, 1], jnp.maximum)
        )
        for place in places:
            top = jnp.maximum(top, fold_rows(s_all[place], jnp.maximum))
        row_top = jnp.max(top, axis=0, keepdims=True)
        mass = jnp.zeros((8, TOK), F32)
        drift = jnp.zeros((8, TOK), F32)
        pairs = [(s_near.at[h, t], dp_near.at[h, t]) for t in range(2)]
        for s_ref, dp_ref in pairs:
            e = jnp.exp(s_ref[...] - row_top)
            mass += fold_rows(e, jnp.add)
            drift += fold_rows(e * dp_ref[...], jnp.add)
        for place in places:
            e = jnp.exp(s_all[place] - row_top)
            mass += fold_rows(e, jnp.add)
            drift += fold_rows(e * dp_all[place], jnp.add)
        whole = jnp.sum(mass, axis=0, keepdims=True)
        lse_ref[h] = jnp.broadcast_to(row_top + jnp.log(whole), (8, TOK))
        delta = jnp.sum(drift, axis=0, keepdims=True) / whole
        delta_ref[h] = jnp.broadcast_to(delta, (8, TOK))
        return carry

    lax.fori_loop(0, NH, stats, 0)

    def xb_copy(r, p):
        slot = plane_of(r) * NP + lax.rem(xc + p, NP)
        return pltpu.make_async_remote_copy(
            src_ref=staged.at[pl.ds(slot * 2, 2)],
            dst_ref=back_x.at[r, p],
            send_sem=xb_send.at[r],
            recv_sem=xb_recv.at[r],
            device_id=in_plane(p),
            device_id_type=MESH,
        )

    def xb_all(r):
        return pltpu.make_async_remote_copy(
            src_ref=back_x.at[r, pl.ds(1, NP - 1)],
            dst_ref=back_x.at[r, pl.ds(1, NP - 1)],
            send_sem=xb_send.at[r],
            recv_sem=xb_recv.at[r],
            device_id=in_plane(1),
            device_id_type=MESH,
        )

    def far_terms(r):
        def term(p):
            slot = plane_of(r) * NP + lax.rem(xc + p, NP)
            code = req_s[xc, 0, slot]
            head = lax.rem(jnp.maximum(code, 0), NH)
            probs = jnp.exp(s_all[slot] - lse_ref[head][:1])
            probs = jnp.where(code >= 0, probs, 0.0)
            ds = (probs * (dp_all[slot] - delta_ref[head][:1]) * FACTOR).astype(BF16)
            ds_all[slot] = ds
            staged[slot * 2] = dot_nn(probs.astype(BF16), g_heads[head]).astype(BF16)
            staged[slot * 2 + 1] = dot_nn(ds, q_heads[head]).astype(BF16)

        def one(p, carry):
            term(p)
            xb_copy(r, p).start()
            return carry

        lax.fori_loop(1, NP, one, 0)
        term(0)

    def zb_copy(d, level, kind, t):
        r = level if d == 0 else NZ - level
        part = pl.ds(t * NH, NH)
        at = ((level - 1) * 2 + kind) * 2 + t
        return pltpu.make_async_remote_copy(
            src_ref=bufs[kind][r].at[part],
            dst_ref=back_z.at[d, level - 1, kind, part],
            send_sem=zb_send.at[d, at],
            recv_sem=zb_recv.at[d, at],
            device_id=z_next[d],
            device_id_type=MESH,
        )

    def summed(r, kind, block):
        slot = plane_of(r) * NP + xc
        acc = jnp.where(
            req_s[xc, 0, slot] == block, staged[slot * 2 + kind].astype(F32), 0.0
        )
        for p in range(1, NP):
            code = req_s[lax.rem(xc + NP - p, NP), 0, slot]
            acc += jnp.where(code == block, back_x[r, p, kind].astype(F32), 0.0)
        return acc

    def pass_on(d, level):
        r = level if d == 0 else NZ - level
        for t in (1 - d, d) if level == 3 else ((d,) if level == 4 else (0, 1)):
            chained = level < 3 or (level == 3 and t == d)
            for kind in range(2):
                if chained:
                    zb_copy(d, level + 1, kind, t).wait_recv()

                def one(b, carry):
                    block = t * NH + b
                    acc = summed(r, kind, block)
                    if chained:
                        acc += back_z[d, level, kind, block].astype(F32)
                    bufs[kind][r][block] = acc.astype(BF16)
                    return carry

                lax.fori_loop(0, NH, one, 0)
                zb_copy(d, level, kind, t).start()

    far_terms(4)
    far_terms(5)
    far_terms(3)
    xb_all(4).wait_recv()
    pass_on(0, 4)
    pass_on(1, 4)
    far_terms(6)
    far_terms(2)
    far_terms(7)
    far_terms(1)
    far_terms(0)

    def head_terms(h, carry):
        dq = jnp.zeros((TOK, HD), F32)
        lse, delta = lse_ref[h][:1], delta_ref[h][:1]
        for t in range(2):
            probs = jnp.exp(s_near[h, t] - lse)
            ds = (probs * (dp_near[h, t] - delta) * FACTOR).astype(BF16)
            dv_sum[t * NH + h] = dot_nn(probs.astype(BF16), g_heads[h])
            dk_sum[t * NH + h] = dot_nn(ds, q_heads[h])
            dq += dot_tn(ds, k_bufs[0][t * NH + h])
        for c in range(REM):
            place = sel[0, h, c] >> 1
            dq += dot_tn(ds_all[place], k_got[place])
        dq_wide[h] = dq
        return carry

    xb_all(5).wait_recv()
    pass_on(1, 3)
    xb_all(3).wait_recv()
    pass_on(0, 3)
    lax.fori_loop(0, NH, head_terms, 0)
    dots = jnp.zeros((TOK, HD), F32)
    for h in range(NH):
        cols = slice(h * HD, (h + 1) * HD)
        dots += q_gain[:, cols] * dq_wide[h] * q_in[:, cols].astype(F32)
    y_start(1, jnp.sum(dots, axis=1, keepdims=True), 0.0)
    for level in (2, 1):
        xb_all(NZ - level).wait_recv()
        pass_on(1, level)
        xb_all(level).wait_recv()
        pass_on(0, level)

    def finish(wide, gain, grad, scale, dot_mean):
        return (scale * gain * grad - wide * (scale * scale * scale) * dot_mean).astype(BF16)

    q_dot, _ = as_columns(y_total(1) / width_all)
    for h in range(NH):
        cols = slice(h * HD, (h + 1) * HD)
        dq_out[:, cols] = finish(
            q_in[:, cols].astype(F32), q_gain[:, cols], dq_wide[h], q_scale_ref[...], q_dot
        )

    xb_all(0).wait_recv()

    def own_sum(block, carry):
        dk_sum[block] += summed(0, 1, block)
        dv_sum[block] += summed(0, 0, block)
        return carry

    lax.fori_loop(0, NT, own_sum, 0)
    for kind in range(2):
        for t in range(2):
            for d in range(2):
                zb_copy(d, 1, kind, t).wait_recv()
    for t in range(2):
        rows = slice(t * TILE, (t + 1) * TILE)
        for h in range(NH):
            cols = slice(h * HD, (h + 1) * HD)
            b = t * NH + h
            dv = dv_sum[b] + back_z[0, 0, 0, b].astype(F32) + back_z[1, 0, 0, b].astype(F32)
            dv_out[rows, cols] = dv.astype(BF16)
            dk_sum[b] = dk_sum[b] + back_z[0, 0, 1, b].astype(F32) + back_z[1, 0, 1, b].astype(F32)
    columns = []
    for t in range(2):
        rows = slice(t * TILE, (t + 1) * TILE)
        dots = jnp.zeros((TILE, HD), F32)
        for h in range(NH):
            cols = slice(h * HD, (h + 1) * HD)
            dots += k_gain[:, cols] * dk_sum[t * NH + h] * k_in[rows, cols].astype(F32)
        columns.append(jnp.sum(dots, axis=1, keepdims=True))
    y_start(2, jnp.concatenate(columns, axis=0), 0.0)
    k_dot, _ = as_columns(y_total(2) / width_all)
    for t in range(2):
        rows = slice(t * TILE, (t + 1) * TILE)
        for h in range(NH):
            cols = slice(h * HD, (h + 1) * HD)
            dk_out[rows, cols] = finish(
                k_in[rows, cols].astype(F32),
                k_gain[:, cols],
                dk_sum[t * NH + h],
                k_scale_ref[rows],
                k_dot[rows],
            )

    for n in range(3):
        for p in range(1, NY):
            y_copy(n, p).wait_send()
    for r in range(NZ):
        xb_all(r).wait_send()
    for level in range(1, 5):
        for kind in range(2):
            for t in range(2):
                for d in range(2):
                    if level < 4 or t == d:
                        zb_copy(d, level, kind, t).wait_send()


def on_device(q_pre, k_pre, values, out_grad, q_gain, k_gain, selected):
    width_dev = q_pre.shape[1]
    width_all = float(width_dev * lax.axis_size("head"))
    vmem = pl.BlockSpec(memory_space=pltpu.VMEM)
    dma = pltpu.SemaphoreType.DMA
    slots = NZ * NP
    scratch = [pltpu.VMEM((NT, TILE, HD), BF16) for _ in range(2 * NZ)] + [
        pltpu.VMEM((2 * slots, TILE, HD), BF16),
        pltpu.VMEM((slots, TILE, HD), BF16),
        pltpu.VMEM((slots, TILE, HD), BF16),
        pltpu.VMEM((slots, TILE, TOK), F32),
        pltpu.VMEM((slots, TILE, TOK), F32),
        pltpu.VMEM((slots, TILE, TOK), BF16),
        pltpu.VMEM((NZ, NP, 2, TILE, HD), BF16),
        pltpu.VMEM((2, 4, 2, NT, TILE, HD), BF16),
        pltpu.VMEM((NH, 2, TILE, TOK), F32),
        pltpu.VMEM((NH, 2, TILE, TOK), F32),
        pltpu.VMEM((NH, TOK, HD), BF16),
        pltpu.VMEM((NH, TOK, HD), BF16),
        pltpu.VMEM((NH, 8, TOK), F32),
        pltpu.VMEM((NH, 8, TOK), F32),
        pltpu.VMEM((NH, TOK, HD), F32),
        pltpu.VMEM((NT, TILE, HD), F32),
        pltpu.VMEM((NT, TILE, HD), F32),
        pltpu.VMEM((TOK, 128), F32),
        pltpu.VMEM((TOK, 128), F32),
        pltpu.VMEM((3, 8, TOK), F32),
        pltpu.VMEM((3, NY - 1, 8, TOK), F32),
        pltpu.VMEM((NP, 8, 128), jnp.int32),
        pltpu.SMEM((NP, 8, 128), jnp.int32),
        dma((2, 16)),
        dma((2, 16)),
        dma((2 * NZ,)),
        dma((2 * NZ,)),
        dma((NZ,)),
        dma((NZ,)),
        dma((2, 16)),
        dma((2, 16)),
        dma((3, NY - 1)),
        dma((3, NY - 1)),
        dma((NP - 1,)),
        dma((NP - 1,)),
        dma((1,)),
    ]
    out = jax.ShapeDtypeStruct(q_pre.shape, BF16)
    return pl.pallas_call(
        functools.partial(kernel, width_all),
        out_shape=(out, out, out),
        in_specs=[pl.BlockSpec(memory_space=pltpu.SMEM)] + [vmem] * 6,
        out_specs=(vmem, vmem, vmem),
        scratch_shapes=scratch,
        compiler_params=pltpu.CompilerParams(
            collective_id=0, has_side_effects=True, vmem_limit_bytes=62 * 2**20
        ),
        name="sparse_attention_backward",
    )(
        selected,
        q_pre,
        k_pre,
        values,
        out_grad,
        q_gain.reshape(1, -1),
        k_gain.reshape(1, -1),
    )


def solution(mesh):
    placed = (
        P("ctx", "head"),
        P("ctx", "head"),
        P("ctx", "head"),
        P("ctx", "head"),
        P("head"),
        P("head"),
        P("ctx", "head", None),
    )
    return jax.shard_map(
        on_device,
        mesh=mesh,
        in_specs=placed,
        out_specs=(P("ctx", "head"), P("ctx", "head"), P("ctx", "head")),
        check_vma=False,
    )
```

time: 411 us -> 152 us (0.37); the launches traced: 405 us -> 152 us
  waiting for transfers between devices: 269 us -> 0 us
  Pallas kernels: 0 us -> 145 us
  local copies, waits for them, and re-layouts: 53.8 us -> 6.73 us
  starting transfers between devices: 33.1 us -> 0 us
  matrix products: 20 us -> 0 us
  blocking collectives: 15 us -> 0 us
  other arithmetic: 13 us -> 0 us
    all_to_all x3 -> x0, waiting for transfers between devices: 269 us -> none  [the longest x1 176 us: on_device(): lax.all_to_all(sending.reshape(n_ctx, capacity, 2, TILE, HD), 'ctx', spli...]
    pallas_call x0 -> x1, Pallas kernels: none -> 145 us  [on_device(): pl.pallas_call(functools.partial(kernel, width_all), out_shape=(out, out,...]
    all_to_all x3 -> x0, starting transfers between devices: 33.1 us -> none  [the longest x1 13 us: on_device(): lax.all_to_all(request.reshape(n_ctx, capacity), 'ctx', split_axis=0, con...]
    dot_general x11 -> x0, matrix products: 20 us -> none  [the longest x1 8.4 us: table_sum(): jnp.dot(taken, flat_pieces, precision=lax.Precision.HIGHEST, preferred_el...]
    psum x2 -> x0, blocking collectives: 15 us -> none  [the longest x1 9.02 us: on_device(): lax.psum((jnp.sum(q_wide * q_wide, axis=1), jnp.sum(k_wide * k_wide, axis...]
    unnamed x37 -> x10, local copies, waits for them, and re-layouts: 17.7 us -> 4.19 us
    scatter x1 -> x0, local copies, waits for them, and re-layouts: 11 us -> none  [on_device(): jnp.zeros((n_buffer, 2, TILE, HD), jnp.float32).at[position].set(grads)]
    gather x4 -> x0, local copies, waits for them, and re-layouts: 9.51 us -> none  [the longest x2 6.39 us: on_device(): slot_kv = incoming[position].reshape(heads_dev, remote_count, 2, TILE, HD)]
  transfers between devices with their start and end apart: 3 -> 0, of which waited for: 2 -> 0; matrix products, arithmetic and copies ran while one was open for 3% -> 0% of each run, Pallas kernels for 0% -> 0%
where the time goes in v1:
time: 152 us
  Pallas kernels  145 us (95%)
  local copies, waits for them, and re-layouts  6.73 us (4%)
    pallas_call x1, Pallas kernels, on_device(): pl.pallas_call(functools.partial(kernel, width_all), out_shape=(out, out,...  145 us
    unnamed x10, local copies, waits for them, and re-layouts  4.19 us

profile of v1, /device:TPU:1, one launch (start us, length us, event | category | flops | bytes accessed | tf_op | source)
XLA Modules:
  0.0 151.9 jit_solution(17340601154281509217)
XLA Ops:
  0.6 0.0 copy-start.2
  0.6 1.3 reshape.12.refs_5_
  1.9 1.3 reshape.13.refs_6_
  3.2 0.0 copy-done.2
  3.2 0.6 copy.10.refs_0_
  3.8 144.5 %sparse_attention_backward.1 = (bf16[256,640]{1,0:T(8,128)(2,1)}, bf16[256,640]{1,0:T(8,128)(2,1)}, bf16[256,640]{1,0:T(8,128)(2,1)}) custom-call(s32[2,5,7]{2,1,0:T(8,128)} %copy.10.refs_0_, bf16[256,640]{1,0:T(8,128)(2,1)} %refs_1_.1, bf16[256,640]{1,0:T(8,128)(2,1)} %refs_2_.1, bf16[256,640]{1,0:T(8,128)(2,1)} %refs_3_.1, bf16[256,640]{1,0:T(8,128)(2,1)} %refs_4_.1, ...), custom_call_target="tpu_custom_call" | custom-call | tf_op jit(solution)/shard_map/sparse_attention_backward/pallas_call | solution.py:580
  148.3 0.0 copy-start.1
  148.3 1.8 %copy.14 = bf16[256,640]{1,0:T(8,128)(2,1)} copy(bf16[256,640]{1,0:T(8,128)(2,1)} %get-tuple-element.6) | data formatting | bytes 655360
  150.1 0.0 copy-done.1
  150.1 0.0 copy-start
  150.1 0.7 copy.15
  150.8 0.4 copy-done
  151.2 0.7 copy.16
Async XLA Ops:
  0.6 2.6 %copy-start.2 = (s32[2,5,7]{2,0,1:T(2,128)S(1)}, s32[2,5,7]{2,0,1:T(2,128)}, u32[]{:S(2)}) copy-start(s32[2,5,7]{2,0,1:T(2,128)} %param.13) | copy-start | bytes 844
  148.3 1.8 %copy-start.1 = (bf16[256,640]{1,0:T(8,128)(2,1)S(1)}, bf16[256,640]{1,0:T(8,128)(2,1)}, u32[]{:S(2)}) copy-start(bf16[256,640]{1,0:T(8,128)(2,1)} %get-tuple-element.7) | copy-start | bytes 983044
  150.1 1.1 copy-start

commit v2 on v0

v2 whole, which is shorter than its diff:
```python
import functools
import math

import jax
import jax.numpy as jnp
from jax import lax
from jax.experimental import pallas as pl
from jax.experimental.pallas import tpu as pltpu
from jax.sharding import PartitionSpec as P

HD = 128
TILE = 128
NH = 5
REM = 7
NT = 2 * NH
NZ = 8
NP = 8
NX = 4
NY = 4
TOK = 2 * TILE
EPS = 1e-6
FACTOR = 1.0 / math.sqrt(HD)
MESH = pl.DeviceIdType.MESH
F32 = jnp.float32
BF16 = jnp.bfloat16


def dot_nt(a, b):
    return lax.dot_general(a, b, (((1,), (1,)), ((), ())), preferred_element_type=F32)


def dot_nn(a, b):
    return lax.dot_general(a, b, (((1,), (0,)), ((), ())), preferred_element_type=F32)


def dot_tn(a, b):
    return lax.dot_general(a, b, (((0,), (0,)), ((), ())), preferred_element_type=F32)


def fold_rows(array, op):
    parts = [array[8 * i : 8 * i + 8] for i in range(array.shape[0] // 8)]
    while len(parts) > 1:
        parts = [op(parts[i], parts[i + 1]) for i in range(0, len(parts), 2)]
    return parts[0]


def kernel(width_all, *refs):
    sel, q_in, k_in, v_in, g_in, q_gain, k_gain, dq_out, dk_out, dv_out = refs[:10]
    scratch = list(refs[10:])
    g_bufs = [scratch.pop(0) for _ in range(NZ)]
    q_bufs = [scratch.pop(0) for _ in range(NZ)]
    moving = (g_bufs, q_bufs)
    (
        v_all,
        k_all,
        s_all,
        dp_all,
        back_z,
        core_out,
        core_in,
        x_out,
        x_in,
        s_near,
        dp_near,
        near_stats,
        stat_out,
        stat_in,
        reply_out,
        reply_in,
        lse_ref,
        delta_ref,
        dq_wide,
        dk_sum,
        dv_sum,
        q_scale_ref,
        k_scale_ref,
        y_out,
        y_in,
        req_v,
        req_s,
        zf_send,
        zf_recv,
        xg_send,
        xg_recv,
        cg_send,
        cg_recv,
        st_send,
        st_recv,
        rp_send,
        rp_recv,
        zb_send,
        zb_recv,
        cb_send,
        cb_recv,
        xb_send,
        xb_recv,
        y_send,
        y_recv,
        rq_send,
        rq_recv,
        here_sem,
    ) = scratch
    fixed = (v_all, k_all)

    me = lax.axis_index("ctx")
    group = lax.axis_index("head")
    z = me // NP
    x = lax.rem(me, NP) // 2
    core = lax.rem(me, 2)

    def along_z(o):
        return {"ctx": lax.rem(z + o, NZ) * NP + lax.rem(me, NP), "head": group}

    def along_x(o):
        return {"ctx": z * NP + lax.rem(x + o, NX) * 2 + core, "head": group}

    def along_y(o):
        return {"ctx": me, "head": lax.rem(group + o, NY)}

    other_core = {"ctx": z * NP + x * 2 + (1 - core), "head": group}
    z_next = (along_z(1), along_z(NZ - 1))
    x_next = (along_x(1), along_x(NX - 1))

    barrier = pltpu.get_barrier_semaphore()
    peers = [along_z(o) for o in range(1, NZ)] + [along_y(o) for o in range(1, NY)]
    peers += [x_next[0], x_next[1], other_core]
    for peer in peers:
        pl.semaphore_signal(barrier, inc=1, device_id=peer, device_id_type=MESH)

    def remote(src, dst, send, recv, to):
        return pltpu.make_async_remote_copy(
            src_ref=src,
            dst_ref=dst,
            send_sem=send,
            recv_sem=recv,
            device_id=to,
            device_id_type=MESH,
        )

    for h in range(NH):
        cols = slice(h * HD, (h + 1) * HD)
        g_bufs[0][h] = g_in[:, cols]
        for t in range(2):
            v_all[t * NH + h] = v_in[t * TILE : (t + 1) * TILE, cols]
    lane = lax.broadcasted_iota(jnp.int32, (8, 128), 1)
    wanted = jnp.full((8, 128), -1, jnp.int32)
    for h in range(NH):
        for c in range(REM):
            tile = sel[h, 0, c]
            wanted = jnp.where(lane == (tile >> 1), (tile & 1) * NH + h, wanted)
    req_v[0] = wanted

    def squares(ref):
        wide = ref[...].astype(F32)
        return jnp.sum(wide * wide, axis=1, keepdims=True)

    lanes_tok = lax.broadcasted_iota(jnp.int32, (TOK, 128), 1)

    def as_rows(first, second):
        both = jnp.where(lanes_tok == 0, first, jnp.where(lanes_tok == 1, second, 0.0))
        return jnp.transpose(both)[:8]

    def as_columns(rows):
        tall = jnp.transpose(jnp.concatenate([rows, jnp.zeros((120, TOK), F32)], axis=0))
        return tall[:, 0:1], tall[:, 1:2]

    def y_copy(n, p):
        return remote(
            y_out.at[n], y_in.at[n, p - 1], y_send.at[n, p - 1], y_recv.at[n, p - 1], along_y(p)
        )

    def y_start(n, first, second):
        y_out[n] = as_rows(first, second)
        for p in range(1, NY):
            y_copy(n, p).start()

    def y_total(n):
        for p in range(1, NY):
            y_copy(n, p).wait_recv()
        return (y_out[n] + y_in[n, 0]) + (y_in[n, 1] + y_in[n, 2])

    q_square, k_square = squares(q_in), squares(k_in)
    pl.semaphore_wait(barrier, len(peers))

    def req_copy(o):
        return remote(
            req_v.at[0], req_v.at[NZ - o], rq_send.at[o - 1], rq_recv.at[o - 1], along_z(o)
        )

    def zf_copy(d, hop, kind, t):
        source = (NZ + 1 - hop) % NZ if d == 0 else hop - 1
        target = NZ - hop if d == 0 else hop
        at = ((hop - 1) * 2 + kind) * 2 + t
        rows = pl.ds(t * TILE, TILE)
        return remote(
            moving[kind][source].at[:, rows],
            moving[kind][target].at[:, rows],
            zf_send.at[d, at],
            zf_recv.at[d, at],
            z_next[d],
        )

    def xg_copy(kind, d, n):
        if n < 2:
            src, dst = n * NH, (6 if d == 0 else 2) * NT + n * NH
        else:
            src = (6 if d == 0 else 2) * NT + d * NH
            dst = 4 * NT + d * NH
        return remote(
            fixed[kind].at[pl.ds(src, NH)],
            fixed[kind].at[pl.ds(dst, NH)],
            xg_send.at[kind, d, n],
            xg_recv.at[kind, d, n],
            x_next[d],
        )

    def cg_copy(kind, dx):
        return remote(
            fixed[kind].at[pl.ds(2 * dx * NT, NT)],
            fixed[kind].at[pl.ds((2 * dx + 1) * NT, NT)],
            cg_send.at[kind, dx],
            cg_recv.at[kind, dx],
            other_core,
        )

    y_start(0, q_square, k_square)
    for t in range(2):
        for d in range(2):
            zf_copy(d, 1, 0, t).start()
            xg_copy(0, d, t).start()
    for o in range(1, NZ):
        req_copy(o).start()
    cg_copy(0, 0).start()

    total = y_total(0)
    q_scale, k_scale = as_columns(lax.rsqrt(total / width_all + EPS))
    q_scale_ref[...] = jnp.broadcast_to(q_scale, (TOK, 128))
    k_scale_ref[...] = jnp.broadcast_to(k_scale, (TOK, 128))

    def gain(ref, h):
        return ref[h * HD : (h + 1) * HD].reshape(1, HD)

    for t in range(2):
        rows = slice(t * TILE, (t + 1) * TILE)
        for h in range(NH):
            cols = slice(h * HD, (h + 1) * HD)
            q_bufs[0][h, rows] = (
                q_in[rows, cols].astype(F32) * q_scale_ref[rows] * gain(q_gain, h)
            ).astype(BF16)
            k_all[t * NH + h] = (
                k_in[rows, cols].astype(F32) * k_scale_ref[rows] * gain(k_gain, h)
            ).astype(BF16)
        for d in range(2):
            zf_copy(d, 1, 1, t).start()
            xg_copy(1, d, t).start()
    cg_copy(1, 0).start()

    for o in range(1, NZ):
        req_copy(o).wait_recv()
    table = pltpu.make_async_copy(req_v, req_s, here_sem.at[0])
    table.start()
    table.wait()

    def code_of(r, place):
        dx, other = place // 2, lax.rem(place, 2)
        lane_at = z * NP + lax.rem(x + dx, NX) * 2 + lax.rem(core + other, 2)
        return req_s[r, 0, lane_at]

    def row_stats(s, dp, top):
        e = jnp.exp(s - top)
        return fold_rows(e, jnp.add), fold_rows(e * dp, jnp.add)

    def near_scores(h, carry):
        tops = []
        for t in range(2):
            s = dot_nt(k_all[t * NH + h], q_bufs[0][h]) * FACTOR
            s_near[h, t] = s
            dp_near[h, t] = dot_nt(v_all[t * NH + h], g_bufs[0][h])
            tops.append(fold_rows(s, jnp.maximum))
        top = jnp.max(jnp.maximum(tops[0], tops[1]), axis=0, keepdims=True)
        first = row_stats(s_near[h, 0], dp_near[h, 0], top)
        second = row_stats(s_near[h, 1], dp_near[h, 1], top)
        mass = jnp.sum(first[0] + second[0], axis=0, keepdims=True)
        drift = jnp.sum(first[1] + second[1], axis=0, keepdims=True)
        near_stats[h, 0] = jnp.broadcast_to(top + jnp.log(mass), (8, TOK))
        near_stats[h, 1] = jnp.broadcast_to(drift / mass, (8, TOK))
        return carry

    def st_copy(r):
        return remote(
            stat_out.at[r], stat_in.at[(NZ - r) % NZ], st_send.at[r], st_recv.at[r], along_z(r)
        )

    sub = lax.broadcasted_iota(jnp.int32, (8, TOK), 0)

    def scores(r):
        def one(i, carry):
            lse8, delta8 = carry
            for half in range(2):
                place = 2 * i + half
                code = jnp.maximum(code_of(r, place), 0)
                head = lax.rem(code, NH)
                s = dot_nt(k_all[place * NT + code], q_bufs[r][head]) * FACTOR
                dp = dot_nt(v_all[place * NT + code], g_bufs[r][head])
                s_all[r * NP + place] = s
                dp_all[r * NP + place] = dp
                top = jnp.max(fold_rows(s, jnp.maximum), axis=0, keepdims=True)
                mass, drift = row_stats(s, dp, top)
                mass = jnp.sum(mass, axis=0, keepdims=True)
                drift = jnp.sum(drift, axis=0, keepdims=True)
                lse8 = jnp.where(sub == place, top + jnp.log(mass), lse8)
                delta8 = jnp.where(sub == place, drift / mass, delta8)
            return lse8, delta8

        zero = jnp.zeros((8, TOK), F32)
        lse8, delta8 = lax.fori_loop(0, NP // 2, one, (zero, zero))
        if r == 0:
            stat_in[0, 0] = lse8
            stat_in[0, 1] = delta8
        else:
            stat_out[r, 0] = lse8
            stat_out[r, 1] = delta8
            st_copy(r).start()

    def forward(hop, kind):
        for t in range(2):
            for d in range(2):
                if hop < 4 or t == d:
                    zf_copy(d, hop, kind, t).wait_recv()
                if hop < 3 or (hop == 3 and t == d):
                    zf_copy(d, hop + 1, kind, t).start()

    def plane_first(kind):
        for t in range(2):
            for d in range(2):
                xg_copy(kind, d, t).wait_recv()
                if t == d:
                    xg_copy(kind, d, 2).start()
        cg_copy(kind, 1).start()
        cg_copy(kind, 3).start()

    def plane_second(kind):
        for d in range(2):
            xg_copy(kind, d, 2).wait_recv()
        cg_copy(kind, 2).start()

    forward(1, 0)
    plane_first(0)
    lax.fori_loop(0, NH, near_scores, 0)
    forward(1, 1)
    plane_first(1)
    plane_second(0)
    forward(2, 0)
    plane_second(1)
    for kind in range(2):
        for dx in range(NX):
            cg_copy(kind, dx).wait_recv()
    scores(0)
    forward(2, 1)
    scores(7)
    scores(1)
    forward(3, 0)
    scores(6)
    scores(2)
    forward(3, 1)
    scores(5)
    forward(4, 0)
    scores(3)
    forward(4, 1)
    scores(4)

    for o in range(1, NZ):
        req_copy(o).wait_send()
    for hop in range(1, 5):
        for kind in range(2):
            for t in range(2):
                for d in range(2):
                    if hop < 4 or t == d:
                        zf_copy(d, hop, kind, t).wait_send()
    for kind in range(2):
        for d in range(2):
            for n in range(3):
                xg_copy(kind, d, n).wait_send()
        for dx in range(NX):
            cg_copy(kind, dx).wait_send()

    row_at = lax.broadcasted_iota(jnp.int32, (NZ * NP, TOK), 0)
    head_at = jnp.full((NZ * NP, TOK), -1, jnp.int32)
    for h in range(NH):
        for c in range(REM):
            owner = sel[h, 0, c] >> 1
            dz = (owner // NP - z + NZ) & (NZ - 1)
            dx = ((owner & (NP - 1)) // 2 - x + NX) & (NX - 1)
            place = dx * 2 + ((owner + core) & 1)
            head_at = jnp.where(row_at == dz * NP + place, h, head_at)
    for r in range(1, NZ):
        st_copy(r).wait_recv()
    pair_lse = jnp.concatenate([stat_in[r, 0] for r in range(NZ)], axis=0)
    pair_delta = jnp.concatenate([stat_in[r, 1] for r in range(NZ)], axis=0)
    for h in range(NH):
        mine = head_at == h
        near_lse, near_delta = near_stats[h, 0, :1], near_stats[h, 1, :1]
        top = jnp.max(jnp.where(mine, pair_lse, -3e38), axis=0, keepdims=True)
        top = jnp.maximum(top, near_lse)
        weight = jnp.where(mine, jnp.exp(pair_lse - top), 0.0)
        near_weight = jnp.exp(near_lse - top)
        whole = jnp.sum(weight, axis=0, keepdims=True) + near_weight
        drift = jnp.where(mine, weight * pair_delta, 0.0)
        drift = jnp.sum(drift, axis=0, keepdims=True) + near_weight * near_delta
        reply_out[pl.ds(h, 1)] = top + jnp.log(whole)
        reply_out[pl.ds(8 + h, 1)] = drift / whole

    def rp_copy(o):
        return remote(
            reply_out, reply_in.at[NZ - o], rp_send.at[o - 1], rp_recv.at[o - 1], along_z(o)
        )

    for o in (4, 3, 5, 2, 6, 1, 7):
        rp_copy(o).start()
    reply_in[0] = reply_out[...]
    for o in range(1, NZ):
        rp_copy(o).wait_recv()
    for r in range(NZ):
        for h in range(NH):
            lse_ref[r * NH + h] = jnp.broadcast_to(reply_in[r, h : h + 1], (8, TOK))
            delta_ref[r * NH + h] = jnp.broadcast_to(reply_in[r, 8 + h : 9 + h], (8, TOK))

    def term(r, place):
        pair = r * NP + place
        asked = code_of(r, place)
        code = jnp.maximum(asked, 0)
        head = lax.rem(code, NH)
        probs = jnp.exp(s_all[pair] - lse_ref[r * NH + head][:1])
        probs = jnp.where(asked >= 0, probs, 0.0)
        ds = (probs * (dp_all[pair] - delta_ref[r * NH + head][:1]) * FACTOR).astype(BF16)
        dv = dot_nn(probs.astype(BF16), g_bufs[r][head])
        dk = dot_nn(ds, q_bufs[r][head])
        dq = dot_tn(ds, k_all[place * NT + code])
        s_all[pair, :, :HD] = dv
        s_all[pair, :, HD:] = dk
        dp_all[pair, :, :HD] = dq[:TILE]
        dp_all[pair, :, HD:] = dq[TILE:]

    def key_sum(place, kind, block):
        cols = slice(kind * HD, (kind + 1) * HD)
        acc = jnp.zeros((TILE, HD), F32)
        for r in range(NZ):
            acc += jnp.where(code_of(r, place) == block, s_all[r * NP + place, :, cols], 0.0)
        return acc

    def query_sum(r, t, h):
        cols = slice(t * TILE, (t + 1) * TILE)
        acc = jnp.zeros((TILE, HD), F32)
        for place in range(NP):
            head = lax.rem(jnp.maximum(code_of(r, place), 0), NH)
            acc += jnp.where(head == h, dp_all[r * NP + place, :, cols], 0.0)
        return acc

    def cb_copy(dx):
        part = pl.ds(dx * 2 * NT, 2 * NT)
        return remote(
            core_out.at[part], core_in.at[part], cb_send.at[dx], cb_recv.at[dx], other_core
        )

    def to_core(dx):
        def one(block, carry):
            for kind in range(2):
                acc = key_sum(2 * dx + 1, kind, block)
                core_out[dx * 2 * NT + kind * NT + block] = acc.astype(BF16)
            return carry

        lax.fori_loop(0, NT, one, 0)
        cb_copy(dx).start()

    def chip_sum(dx, kind, block):
        near = core_in[dx * 2 * NT + kind * NT + block].astype(F32)
        return key_sum(2 * dx, kind, block) + near

    def xb_copy(level, d, kind, t):
        dx = 2 if level == 2 else (1 if d == 0 else 3)
        part = pl.ds(kind * NT + t * NH, NH)
        return remote(
            x_out.at[dx - 1, part],
            x_in.at[level - 1, d, part],
            xb_send.at[level - 1, d, kind, t],
            xb_recv.at[level - 1, d, kind, t],
            x_next[d],
        )

    def x_pass(level, d, t):
        dx = 2 if level == 2 else (1 if d == 0 else 3)
        chained = level == 1 and t == d
        for kind in range(2):
            if chained:
                xb_copy(2, d, kind, t).wait_recv()

            def one(b, carry):
                block = t * NH + b
                acc = chip_sum(dx, kind, block)
                if chained:
                    acc += x_in[1, d, kind * NT + block].astype(F32)
                x_out[dx - 1, kind * NT + block] = acc.astype(BF16)
                return carry

            lax.fori_loop(0, NH, one, 0)
            xb_copy(level, d, kind, t).start()

    def zb_copy(d, level, t):
        r = level if d == 0 else NZ - level
        rows = pl.ds(t * TILE, TILE)
        return remote(
            q_bufs[r].at[:, rows],
            back_z.at[d, level - 1, :, rows],
            zb_send.at[d, level - 1, t],
            zb_recv.at[d, level - 1, t],
            z_next[d],
        )

    def z_pass(d, level):
        r = level if d == 0 else NZ - level
        for t in (1 - d, d) if level == 3 else ((d,) if level == 4 else (0, 1)):
            chained = level < 3 or (level == 3 and t == d)
            rows = slice(t * TILE, (t + 1) * TILE)
            if chained:
                zb_copy(d, level + 1, t).wait_recv()

            def one(h, carry):
                acc = query_sum(r, t, h)
                if chained:
                    acc += back_z[d, level, h, rows].astype(F32)
                q_bufs[r][h, rows] = acc.astype(BF16)
                return carry

            lax.fori_loop(0, NH, one, 0)
            zb_copy(d, level, t).start()

    def rest_terms(r):
        def one(i, carry):
            for half in range(2):
                place = 2 * i + half
                term(r, place + jnp.where(i >= 2, 2, 0))
            return carry

        lax.fori_loop(0, NP // 2 - 1, one, 0)

    for r in range(NZ):
        term(r, 5)
    to_core(2)
    for r in range(NZ):
        term(r, 4)
    rest_terms(4)
    z_pass(0, 4)
    z_pass(1, 4)
    cb_copy(2).wait_recv()
    x_pass(2, 0, 0)
    x_pass(2, 1, 1)
    rest_terms(5)
    z_pass(1, 3)
    rest_terms(3)
    z_pass(0, 3)
    for r in (6, 2, 7, 1, 0):
        rest_terms(r)
    to_core(1)
    to_core(3)
    cb_copy(1).wait_recv()
    x_pass(1, 0, 1)
    cb_copy(3).wait_recv()
    x_pass(1, 1, 0)
    z_pass(1, 2)
    z_pass(0, 2)
    x_pass(1, 0, 0)
    x_pass(1, 1, 1)
    to_core(0)
    z_pass(1, 1)
    z_pass(0, 1)

    def near_terms(h, carry):
        dq = jnp.zeros((TOK, HD), F32)
        lse, delta = lse_ref[h][:1], delta_ref[h][:1]
        for t in range(2):
            probs = jnp.exp(s_near[h, t] - lse)
            ds = (probs * (dp_near[h, t] - delta) * FACTOR).astype(BF16)
            dv_sum[t * NH + h] = dot_nn(probs.astype(BF16), g_bufs[0][h])
            dk_sum[t * NH + h] = dot_nn(ds, q_bufs[0][h])
            dq += dot_tn(ds, k_all[t * NH + h])
        dq_wide[h] = dq
        for t in range(2):
            dq_wide[h, t * TILE : (t + 1) * TILE] += query_sum(0, t, h)
        return carry

    lax.fori_loop(0, NH, near_terms, 0)
    cb_copy(0).wait_recv()

    def own_sum(block, carry):
        dv_sum[block] += chip_sum(0, 0, block)
        dk_sum[block] += chip_sum(0, 1, block)
        return carry

    lax.fori_loop(0, NT, own_sum, 0)

    for t in range(2):
        for d in range(2):
            zb_copy(d, 1, t).wait_recv()
    dots = jnp.zeros((TOK, HD), F32)
    for h in range(NH):
        cols = slice(h * HD, (h + 1) * HD)
        dq = dq_wide[h] + back_z[0, 0, h].astype(F32) + back_z[1, 0, h].astype(F32)
        dq_wide[h] = dq
        dots += gain(q_gain, h) * dq * q_in[:, cols].astype(F32)
    q_dot = jnp.sum(dots, axis=1, keepdims=True)

    for t in range(2):
        for d in range(2):
            for kind in range(2):
                xb_copy(1, d, kind, t).wait_recv()
    columns = []
    for t in range(2):
        rows = slice(t * TILE, (t + 1) * TILE)
        dots = jnp.zeros((TILE, HD), F32)
        for h in range(NH):
            cols = slice(h * HD, (h + 1) * HD)
            b = t * NH + h
            dv = dv_sum[b] + x_in[0, 0, b].astype(F32) + x_in[0, 1, b].astype(F32)
            dv_out[rows, cols] = dv.astype(BF16)
            dk = dk_sum[b] + x_in[0, 0, NT + b].astype(F32) + x_in[0, 1, NT + b].astype(F32)
            dk_sum[b] = dk
            dots += gain(k_gain, h) * dk * k_in[rows, cols].astype(F32)
        columns.append(jnp.sum(dots, axis=1, keepdims=True))
    y_start(1, q_dot, jnp.concatenate(columns, axis=0))

    def finish(wide, gains, grad, scale, dot_mean):
        return (scale * gains * grad - wide * (scale * scale * scale) * dot_mean).astype(BF16)

    q_dot, k_dot = as_columns(y_total(1) / width_all)
    for h in range(NH):
        cols = slice(h * HD, (h + 1) * HD)
        dq_out[:, cols] = finish(
            q_in[:, cols].astype(F32), gain(q_gain, h), dq_wide[h], q_scale_ref[...], q_dot
        )
        for t in range(2):
            rows = slice(t * TILE, (t + 1) * TILE)
            dk_out[rows, cols] = finish(
                k_in[rows, cols].astype(F32),
                gain(k_gain, h),
                dk_sum[t * NH + h],
                k_scale_ref[rows],
                k_dot[rows],
            )

    for n in range(2):
        for p in range(1, NY):
            y_copy(n, p).wait_send()
    for r in range(1, NZ):
        st_copy(r).wait_send()
        rp_copy(r).wait_send()
    for dx in range(NX):
        cb_copy(dx).wait_send()
    for t in range(2):
        for d in range(2):
            for level in range(1, 5):
                if level < 4 or t == d:
                    zb_copy(d, level, t).wait_send()
            for kind in range(2):
                xb_copy(1, d, kind, t).wait_send()
                if t == d:
                    xb_copy(2, d, kind, t).wait_send()


def on_device(q_pre, k_pre, values, out_grad, q_gain, k_gain, selected):
    width_dev = q_pre.shape[1]
    width_all = float(width_dev * lax.axis_size("head"))
    vmem = pl.BlockSpec(memory_space=pltpu.VMEM)
    dma = pltpu.SemaphoreType.DMA
    pairs = NZ * NP
    scratch = [pltpu.VMEM((NH, TOK, HD), BF16) for _ in range(2 * NZ)] + [
        pltpu.VMEM((NP * NT, TILE, HD), BF16),
        pltpu.VMEM((NP * NT, TILE, HD), BF16),
        pltpu.VMEM((pairs, TILE, TOK), F32),
        pltpu.VMEM((pairs, TILE, TOK), F32),
        pltpu.VMEM((2, 4, NH, TOK, HD), BF16),
        pltpu.VMEM((NX * 2 * NT, TILE, HD), BF16),
        pltpu.VMEM((NX * 2 * NT, TILE, HD), BF16),
        pltpu.VMEM((3, 2 * NT, TILE, HD), BF16),
        pltpu.VMEM((2, 2, 2 * NT, TILE, HD), BF16),
        pltpu.VMEM((NH, 2, TILE, TOK), F32),
        pltpu.VMEM((NH, 2, TILE, TOK), F32),
        pltpu.VMEM((NH, 2, 8, TOK), F32),
        pltpu.VMEM((NZ, 2, NP, TOK), F32),
        pltpu.VMEM((NZ, 2, NP, TOK), F32),
        pltpu.VMEM((16, TOK), F32),
        pltpu.VMEM((NZ, 16, TOK), F32),
        pltpu.VMEM((NZ * NH, 8, TOK), F32),
        pltpu.VMEM((NZ * NH, 8, TOK), F32),
        pltpu.VMEM((NH, TOK, HD), F32),
        pltpu.VMEM((NT, TILE, HD), F32),
        pltpu.VMEM((NT, TILE, HD), F32),
        pltpu.VMEM((TOK, 128), F32),
        pltpu.VMEM((TOK, 128), F32),
        pltpu.VMEM((2, 8, TOK), F32),
        pltpu.VMEM((2, NY - 1, 8, TOK), F32),
        pltpu.VMEM((NZ, 8, 128), jnp.int32),
        pltpu.SMEM((NZ, 8, 128), jnp.int32),
        dma((2, 16)),
        dma((2, 16)),
        dma((2, 2, 3)),
        dma((2, 2, 3)),
        dma((2, NX)),
        dma((2, NX)),
        dma((NZ,)),
        dma((NZ,)),
        dma((NZ - 1,)),
        dma((NZ - 1,)),
        dma((2, 4, 2)),
        dma((2, 4, 2)),
        dma((NX,)),
        dma((NX,)),
        dma((2, 2, 2, 2)),
        dma((2, 2, 2, 2)),
        dma((2, NY - 1)),
        dma((2, NY - 1)),
        dma((NZ - 1,)),
        dma((NZ - 1,)),
        dma((1,)),
    ]
    out = jax.ShapeDtypeStruct(q_pre.shape, BF16)
    return pl.pallas_call(
        functools.partial(kernel, width_all),
        out_shape=(out, out, out),
        in_specs=[pl.BlockSpec(memory_space=pltpu.SMEM)] + [vmem] * 6,
        out_specs=(vmem, vmem, vmem),
        scratch_shapes=scratch,
        compiler_params=pltpu.CompilerParams(
            collective_id=0, has_side_effects=True, vmem_limit_bytes=60 * 2**20
        ),
        name="sparse_attention_backward",
    )(
        jnp.transpose(selected, (1, 0, 2)), q_pre, k_pre, values, out_grad, q_gain, k_gain
    )


def solution(mesh):
    placed = (
        P("ctx", "head"),
        P("ctx", "head"),
        P("ctx", "head"),
        P("ctx", "head"),
        P("head"),
        P("head"),
        P("ctx", "head", None),
    )
    return jax.shard_map(
        on_device,
        mesh=mesh,
        in_specs=placed,
        out_specs=(P("ctx", "head"), P("ctx", "head"), P("ctx", "head")),
        check_vma=False,
    )
```

time: 411 us -> 124 us (0.30); the launches traced: 405 us -> 123 us
  waiting for transfers between devices: 269 us -> 0 us
  Pallas kernels: 0 us -> 119 us
  local copies, waits for them, and re-layouts: 53.8 us -> 3.59 us
  starting transfers between devices: 33.1 us -> 0 us
  matrix products: 20 us -> 0 us
  blocking collectives: 15 us -> 0 us
  other arithmetic: 13 us -> 0 us
    all_to_all x3 -> x0, waiting for transfers between devices: 269 us -> none  [the longest x1 176 us: on_device(): lax.all_to_all(sending.reshape(n_ctx, capacity, 2, TILE, HD), 'ctx', spli...]
    pallas_call x0 -> x1, Pallas kernels: none -> 119 us  [on_device(): pl.pallas_call(functools.partial(kernel, width_all), out_shape=(out, out,...]
    all_to_all x3 -> x0, starting transfers between devices: 33.1 us -> none  [the longest x1 13 us: on_device(): lax.all_to_all(request.reshape(n_ctx, capacity), 'ctx', split_axis=0, con...]
    dot_general x11 -> x0, matrix products: 20 us -> none  [the longest x1 8.4 us: table_sum(): jnp.dot(taken, flat_pieces, precision=lax.Precision.HIGHEST, preferred_el...]
    psum x2 -> x0, blocking collectives: 15 us -> none  [the longest x1 9.02 us: on_device(): lax.psum((jnp.sum(q_wide * q_wide, axis=1), jnp.sum(k_wide * k_wide, axis...]
    unnamed x37 -> x7, local copies, waits for them, and re-layouts: 17.7 us -> 3.59 us
    scatter x1 -> x0, local copies, waits for them, and re-layouts: 11 us -> none  [on_device(): jnp.zeros((n_buffer, 2, TILE, HD), jnp.float32).at[position].set(grads)]
    gather x4 -> x0, local copies, waits for them, and re-layouts: 9.51 us -> none  [the longest x2 6.39 us: on_device(): slot_kv = incoming[position].reshape(heads_dev, remote_count, 2, TILE, HD)]
  transfers between devices with their start and end apart: 3 -> 0, of which waited for: 2 -> 0; matrix products, arithmetic and copies ran while one was open for 3% -> 0% of each run, Pallas kernels for 0% -> 0%
where the time goes in v2:
time: 124 us; the launch traced here: 123 us
  Pallas kernels  119 us (96%)
  local copies, waits for them, and re-layouts  3.59 us (3%)
    pallas_call x1, Pallas kernels, on_device(): pl.pallas_call(functools.partial(kernel, width_all), out_shape=(out, out,...  119 us
    unnamed x7, local copies, waits for them, and re-layouts  3.59 us

profile of v2, /device:TPU:1, one launch (start us, length us, event | category | flops | bytes accessed | tf_op | source)
XLA Modules:
  0.0 123.4 jit_solution(1529558628862411699)
XLA Ops:
  0.6 119.2 %sparse_attention_backward.1 = (bf16[256,640]{1,0:T(8,128)(2,1)}, bf16[256,640]{1,0:T(8,128)(2,1)}, bf16[256,640]{1,0:T(8,128)(2,1)}) custom-call(s32[5,2,7]{2,1,0:T(2,128)} %bitcast.1, bf16[256,640]{1,0:T(8,128)(2,1)} %refs_1_.1, bf16[256,640]{1,0:T(8,128)(2,1)} %refs_2_.1, bf16[256,640]{1,0:T(8,128)(2,1)} %refs_3_.1, bf16[256,640]{1,0:T(8,128)(2,1)} %refs_4_.1, ...), custom_call_target="tpu_custom_call" | custom-call | tf_op jit(solution)/shard_map/sparse_attention_backward/pallas_call | solution.py:726
  119.8 0.0 copy-start.1
  119.8 1.8 %copy.13 = bf16[256,640]{1,0:T(8,128)(2,1)} copy(bf16[256,640]{1,0:T(8,128)(2,1)} %get-tuple-element.6) | data formatting | bytes 655360
  121.6 0.0 copy-done.1
  121.6 0.0 copy-start
  121.6 0.7 copy.14
  122.3 0.4 copy-done
  122.7 0.7 copy.15
Async XLA Ops:
  119.8 1.8 %copy-start.1 = (bf16[256,640]{1,0:T(8,128)(2,1)S(1)}, bf16[256,640]{1,0:T(8,128)(2,1)}, u32[]{:S(2)}) copy-start(bf16[256,640]{1,0:T(8,128)(2,1)} %get-tuple-element.7) | copy-start | bytes 983044
  121.6 1.1 copy-start

commit v3 on v2

--- a/solution.py
+++ b/solution.py
@@ -55,6 +55,8 @@
         k_all,
         s_all,
         dp_all,
+        kv_terms,
+        q_terms,
         back_z,
         core_out,
         core_in,
@@ -169,8 +171,7 @@
             y_out.at[n], y_in.at[n, p - 1], y_send.at[n, p - 1], y_recv.at[n, p - 1], along_y(p)
         )
 
-    def y_start(n, first, second):
-        y_out[n] = as_rows(first, second)
+    def y_start(n):
         for p in range(1, NY):
             y_copy(n, p).start()
 
@@ -179,7 +180,7 @@
             y_copy(n, p).wait_recv()
         return (y_out[n] + y_in[n, 0]) + (y_in[n, 1] + y_in[n, 2])
 
-    q_square, k_square = squares(q_in), squares(k_in)
+    y_out[0] = as_rows(squares(q_in), squares(k_in))
     pl.semaphore_wait(barrier, len(peers))
 
     def req_copy(o):
@@ -223,7 +224,7 @@
             other_core,
         )
 
-    y_start(0, q_square, k_square)
+    y_start(0)
     for t in range(2):
         for d in range(2):
             zf_copy(d, 1, 0, t).start()
@@ -293,7 +294,19 @@
 
     sub = lax.broadcasted_iota(jnp.int32, (8, TOK), 0)
 
-    def scores(r):
+    def gradient_scores(r):
+        def one(i, carry):
+            for half in range(2):
+                place = 2 * i + half
+                code = jnp.maximum(code_of(r, place), 0)
+                dp_all[r * NP + place] = dot_nt(
+                    v_all[place * NT + code], g_bufs[r][lax.rem(code, NH)]
+                )
+            return carry
+
+        lax.fori_loop(0, NP // 2, one, 0)
+
+    def scores(r, with_dp=True):
         def one(i, carry):
             lse8, delta8 = carry
             for half in range(2):
@@ -301,9 +314,12 @@
                 code = jnp.maximum(code_of(r, place), 0)
                 head = lax.rem(code, NH)
                 s = dot_nt(k_all[place * NT + code], q_bufs[r][head]) * FACTOR
-                dp = dot_nt(v_all[place * NT + code], g_bufs[r][head])
+                if with_dp:
+                    dp = dot_nt(v_all[place * NT + code], g_bufs[r][head])
+                    dp_all[r * NP + place] = dp
+                else:
+                    dp = dp_all[r * NP + place]
                 s_all[r * NP + place] = s
-                dp_all[r * NP + place] = dp
                 top = jnp.max(fold_rows(s, jnp.maximum), axis=0, keepdims=True)
                 mass, drift = row_stats(s, dp, top)
                 mass = jnp.sum(mass, axis=0, keepdims=True)
@@ -366,8 +382,9 @@
     scores(5)
     forward(4, 0)
     scores(3)
+    gradient_scores(4)
     forward(4, 1)
-    scores(4)
+    scores(4, with_dp=False)
 
     for o in range(1, NZ):
         req_copy(o).wait_send()
@@ -436,25 +453,39 @@
         dv = dot_nn(probs.astype(BF16), g_bufs[r][head])
         dk = dot_nn(ds, q_bufs[r][head])
         dq = dot_tn(ds, k_all[place * NT + code])
-        s_all[pair, :, :HD] = dv
-        s_all[pair, :, HD:] = dk
-        dp_all[pair, :, :HD] = dq[:TILE]
-        dp_all[pair, :, HD:] = dq[TILE:]
+        kv_terms[2 * pair] = dv.astype(BF16)
+        kv_terms[2 * pair + 1] = dk.astype(BF16)
+        q_terms[pair] = dq.astype(BF16)
+
+    zero_tile = jnp.zeros((TILE, HD), BF16)
+
+    def tree(parts):
+        while len(parts) > 1:
+            parts = [parts[i] + parts[i + 1] for i in range(0, len(parts), 2)]
+        return parts[0].astype(F32)
 
     def key_sum(place, kind, block):
-        cols = slice(kind * HD, (kind + 1) * HD)
-        acc = jnp.zeros((TILE, HD), F32)
-        for r in range(NZ):
-            acc += jnp.where(code_of(r, place) == block, s_all[r * NP + place, :, cols], 0.0)
-        return acc
+        return tree(
+            [
+                jnp.where(
+                    code_of(r, place) == block, kv_terms[2 * (r * NP + place) + kind], zero_tile
+                )
+                for r in range(NZ)
+            ]
+        )
 
     def query_sum(r, t, h):
-        cols = slice(t * TILE, (t + 1) * TILE)
-        acc = jnp.zeros((TILE, HD), F32)
-        for place in range(NP):
-            head = lax.rem(jnp.maximum(code_of(r, place), 0), NH)
-            acc += jnp.where(head == h, dp_all[r * NP + place, :, cols], 0.0)
-        return acc
+        rows = slice(t * TILE, (t + 1) * TILE)
+        return tree(
+            [
+                jnp.where(
+                    lax.rem(jnp.maximum(code_of(r, place), 0), NH) == h,
+                    q_terms[r * NP + place, rows],
+                    zero_tile,
+                )
+                for place in range(NP)
+            ]
+        )
 
     def cb_copy(dx):
         part = pl.ds(dx * 2 * NT, 2 * NT)
@@ -543,36 +574,37 @@
 
         lax.fori_loop(0, NP // 2 - 1, one, 0)
 
-    for r in range(NZ):
+    def opposite_terms(r):
+        term(r, 4)
         term(r, 5)
-    to_core(2)
-    for r in range(NZ):
-        term(r, 4)
+
+    opposite_terms(4)
     rest_terms(4)
     z_pass(0, 4)
     z_pass(1, 4)
-    cb_copy(2).wait_recv()
-    x_pass(2, 0, 0)
-    x_pass(2, 1, 1)
+    for r in (5, 3, 6, 2, 7, 1, 0):
+        opposite_terms(r)
+    to_core(2)
     rest_terms(5)
     z_pass(1, 3)
     rest_terms(3)
     z_pass(0, 3)
+    cb_copy(2).wait_recv()
+    x_pass(2, 0, 0)
+    x_pass(2, 1, 1)
     for r in (6, 2, 7, 1, 0):
         rest_terms(r)
     to_core(1)
     to_core(3)
+    z_pass(1, 2)
+    z_pass(0, 2)
     cb_copy(1).wait_recv()
     x_pass(1, 0, 1)
     cb_copy(3).wait_recv()
     x_pass(1, 1, 0)
-    z_pass(1, 2)
-    z_pass(0, 2)
     x_pass(1, 0, 0)
     x_pass(1, 1, 1)
     to_core(0)
-    z_pass(1, 1)
-    z_pass(0, 1)
 
     def near_terms(h, carry):
         dq = jnp.zeros((TOK, HD), F32)
@@ -589,6 +621,8 @@
         return carry
 
     lax.fori_loop(0, NH, near_terms, 0)
+    z_pass(1, 1)
+    z_pass(0, 1)
     cb_copy(0).wait_recv()
 
     def own_sum(block, carry):
@@ -626,7 +660,8 @@
             dk_sum[b] = dk
             dots += gain(k_gain, h) * dk * k_in[rows, cols].astype(F32)
         columns.append(jnp.sum(dots, axis=1, keepdims=True))
-    y_start(1, q_dot, jnp.concatenate(columns, axis=0))
+    y_out[1] = as_rows(q_dot, jnp.concatenate(columns, axis=0))
+    y_start(1)
 
     def finish(wide, gains, grad, scale, dot_mean):
         return (scale * gains * grad - wide * (scale * scale * scale) * dot_mean).astype(BF16)
@@ -666,6 +701,17 @@
                     xb_copy(2, d, kind, t).wait_send()
 
 
+def place_results(a, b, c, a_out, b_out, c_out, sems):
+    copies = [
+        pltpu.make_async_copy(src, dst, sems.at[i])
+        for i, (src, dst) in enumerate(((a, a_out), (b, b_out), (c, c_out)))
+    ]
+    for copy in copies:
+        copy.start()
+    for copy in copies:
+        copy.wait()
+
+
 def on_device(q_pre, k_pre, values, out_grad, q_gain, k_gain, selected):
     width_dev = q_pre.shape[1]
     width_all = float(width_dev * lax.axis_size("head"))
@@ -677,6 +723,8 @@
         pltpu.VMEM((NP * NT, TILE, HD), BF16),
         pltpu.VMEM((pairs, TILE, TOK), F32),
         pltpu.VMEM((pairs, TILE, TOK), F32),
+        pltpu.VMEM((2 * pairs, TILE, HD), BF16),
+        pltpu.VMEM((pairs, TOK, HD), BF16),
         pltpu.VMEM((2, 4, NH, TOK, HD), BF16),
         pltpu.VMEM((NX * 2 * NT, TILE, HD), BF16),
         pltpu.VMEM((NX * 2 * NT, TILE, HD), BF16),
@@ -723,7 +771,7 @@
         dma((1,)),
     ]
     out = jax.ShapeDtypeStruct(q_pre.shape, BF16)
-    return pl.pallas_call(
+    results = pl.pallas_call(
         functools.partial(kernel, width_all),
         out_shape=(out, out, out),
         in_specs=[pl.BlockSpec(memory_space=pltpu.SMEM)] + [vmem] * 6,
@@ -736,6 +784,15 @@
     )(
         jnp.transpose(selected, (1, 0, 2)), q_pre, k_pre, values, out_grad, q_gain, k_gain
     )
+    anywhere = pl.BlockSpec(memory_space=pl.ANY)
+    return pl.pallas_call(
+        place_results,
+        out_shape=(out, out, out),
+        in_specs=[anywhere] * 3,
+        out_specs=(anywhere,) * 3,
+        scratch_shapes=[dma((3,))],
+        name="place_results",
+    )(*results)
 
 
 def solution(mesh):

time: 124 us -> 149 us (1.20)
  Pallas kernels: 119 us -> 148 us
  local copies, waits for them, and re-layouts: 3.59 us -> 0 us
    pallas_call x0 -> x1, Pallas kernels: none -> 30.9 us  [on_device(): pl.pallas_call(place_results, out_shape=(out, out, out), in_specs=[anywhe...]
    unnamed x7 -> x0, local copies, waits for them, and re-layouts: 3.59 us -> none
    pallas_call x1, Pallas kernels: 119 us -> 117 us  [on_device(): pl.pallas_call(functools.partial(kernel, width_all), out_shape=(out, out,...]
where the time goes in v3:
time: 149 us
  Pallas kernels  148 us (99%)
    pallas_call x1, Pallas kernels, on_device(): pl.pallas_call(functools.partial(kernel, width_all), out_shape=(out, out,...  117 us
    pallas_call x1, Pallas kernels, on_device(): pl.pallas_call(place_results, out_shape=(out, out, out), in_specs=[anywhe...  30.9 us

profile of v3, /device:TPU:1, one launch (start us, length us, event | category | flops | bytes accessed | tf_op | source)
XLA Modules:
  0.0 148.7 jit_solution(5886608999284878437)
XLA Ops:
  0.6 117.2 %sparse_attention_backward.1 = (bf16[256,640]{1,0:T(8,128)(2,1)}, bf16[256,640]{1,0:T(8,128)(2,1)}, bf16[256,640]{1,0:T(8,128)(2,1)}) custom-call(s32[5,2,7]{2,1,0:T(2,128)} %bitcast.1, bf16[256,640]{1,0:T(8,128)(2,1)} %refs_1_.1, bf16[256,640]{1,0:T(8,128)(2,1)} %refs_2_.1, bf16[256,640]{1,0:T(8,128)(2,1)} %refs_3_.1, bf16[256,640]{1,0:T(8,128)(2,1)} %refs_4_.1, ...), custom_call_target="tpu_custom_call" | custom-call | tf_op jit(solution)/shard_map/sparse_attention_backward/pallas_call | solution.py:774
  117.8 30.9 %place_results.1 = (bf16[256,640]{1,0:T(8,128)(2,1)}, bf16[256,640]{1,0:T(8,128)(2,1)}, bf16[256,640]{1,0:T(8,128)(2,1)}) custom-call(bf16[256,640]{1,0:T(8,128)(2,1)} %get-tuple-element.6.a, bf16[256,640]{1,0:T(8,128)(2,1)} %get-tuple-element.7.b, bf16[256,640]{1,0:T(8,128)(2,1)} %get-tuple-element.8.c), custom_call_target="tpu_custom_call" | custom-call | tf_op jit(solution)/shard_map/place_results/pallas_call | solution.py:788

commit v4 on v3

--- a/solution.py
+++ b/solution.py
@@ -140,10 +140,89 @@
         )
 
     for h in range(NH):
-        cols = slice(h * HD, (h + 1) * HD)
-        g_bufs[0][h] = g_in[:, cols]
-        for t in range(2):
-            v_all[t * NH + h] = v_in[t * TILE : (t + 1) * TILE, cols]
+        g_bufs[0][h] = g_in[:, h * HD : (h + 1) * HD]
+    pl.semaphore_wait(barrier, len(peers))
+
+    def squares(ref):
+        wide = ref[...].astype(F32)
+        return jnp.sum(wide * wide, axis=1, keepdims=True)
+
+    lanes_tok = lax.broadcasted_iota(jnp.int32, (TOK, 128), 1)
+
+    def as_rows(first, second):
+        both = jnp.where(lanes_tok == 0, first, jnp.where(lanes_tok == 1, second, 0.0))
+        return jnp.transpose(both)[:8]
+
+    def as_columns(rows):
+        tall = jnp.transpose(jnp.concatenate([rows, jnp.zeros((120, TOK), F32)], axis=0))
+        return tall[:, 0:1], tall[:, 1:2]
+
+    def y_copy(n, p):
+        return remote(
+            y_out.at[n], y_in.at[n, p - 1], y_send.at[n, p - 1], y_recv.at[n, p - 1], along_y(p)
+        )
+
+    def y_start(n):
+        for p in range(1, NY):
+            y_copy(n, p).start()
+
+    def y_total(n):
+        for p in range(1, NY):
+            y_copy(n, p).wait_recv()
+        return (y_out[n] + y_in[n, 0]) + (y_in[n, 1] + y_in[n, 2])
+
+    def req_copy(o):
+        return remote(
+            req_v.at[0], req_v.at[NZ - o], rq_send.at[o - 1], rq_recv.at[o - 1], along_z(o)
+        )
+
+    def zf_copy(d, hop, kind, t):
+        source = (NZ + 1 - hop) % NZ if d == 0 else hop - 1
+        target = NZ - hop if d == 0 else hop
+        at = ((hop - 1) * 2 + kind) * 2 + t
+        rows = pl.ds(t * TILE, TILE)
+        return remote(
+            moving[kind][source].at[:, rows],
+            moving[kind][target].at[:, rows],
+            zf_send.at[d, at],
+            zf_recv.at[d, at],
+            z_next[d],
+        )
+
+    def xg_copy(kind, d, n):
+        if n < 2:
+            src, dst = n * NH, (6 if d == 0 else 2) * NT + n * NH
+        else:
+            src = (6 if d == 0 else 2) * NT + d * NH
+            dst = 4 * NT + d * NH
+        return remote(
+            fixed[kind].at[pl.ds(src, NH)],
+            fixed[kind].at[pl.ds(dst, NH)],
+            xg_send.at[kind, d, n],
+            xg_recv.at[kind, d, n],
+            x_next[d],
+        )
+
+    def cg_copy(kind, dx):
+        return remote(
+            fixed[kind].at[pl.ds(2 * dx * NT, NT)],
+            fixed[kind].at[pl.ds((2 * dx + 1) * NT, NT)],
+            cg_send.at[kind, dx],
+            cg_recv.at[kind, dx],
+            other_core,
+        )
+
+    for t in range(2):
+        for d in range(2):
+            zf_copy(d, 1, 0, t).start()
+    y_out[0] = as_rows(squares(q_in), squares(k_in))
+    y_start(0)
+    for t in range(2):
+        for h in range(NH):
+            v_all[t * NH + h] = v_in[t * TILE : (t + 1) * TILE, h * HD : (h + 1) * HD]
+        for d in range(2):
+            xg_copy(0, d, t).start()
+    cg_copy(0, 0).start()
     lane = lax.broadcasted_iota(jnp.int32, (8, 128), 1)
     wanted = jnp.full((8, 128), -1, jnp.int32)
     for h in range(NH):
@@ -151,87 +230,8 @@
             tile = sel[h, 0, c]
             wanted = jnp.where(lane == (tile >> 1), (tile & 1) * NH + h, wanted)
     req_v[0] = wanted
-
-    def squares(ref):
-        wide = ref[...].astype(F32)
-        return jnp.sum(wide * wide, axis=1, keepdims=True)
-
-    lanes_tok = lax.broadcasted_iota(jnp.int32, (TOK, 128), 1)
-
-    def as_rows(first, second):
-        both = jnp.where(lanes_tok == 0, first, jnp.where(lanes_tok == 1, second, 0.0))
-        return jnp.transpose(both)[:8]
-
-    def as_columns(rows):
-        tall = jnp.transpose(jnp.concatenate([rows, jnp.zeros((120, TOK), F32)], axis=0))
-        return tall[:, 0:1], tall[:, 1:2]
-
-    def y_copy(n, p):
-        return remote(
-            y_out.at[n], y_in.at[n, p - 1], y_send.at[n, p - 1], y_recv.at[n, p - 1], along_y(p)
-        )
-
-    def y_start(n):
-        for p in range(1, NY):
-            y_copy(n, p).start()
-
-    def y_total(n):
-        for p in range(1, NY):
-            y_copy(n, p).wait_recv()
-        return (y_out[n] + y_in[n, 0]) + (y_in[n, 1] + y_in[n, 2])
-
-    y_out[0] = as_rows(squares(q_in), squares(k_in))
-    pl.semaphore_wait(barrier, len(peers))
-
-    def req_copy(o):
-        return remote(
-            req_v.at[0], req_v.at[NZ - o], rq_send.at[o - 1], rq_recv.at[o - 1], along_z(o)
-        )
-
-    def zf_copy(d, hop, kind, t):
-        source = (NZ + 1 - hop) % NZ if d == 0 else hop - 1
-        target = NZ - hop if d == 0 else hop
-        at = ((hop - 1) * 2 + kind) * 2 + t
-        rows = pl.ds(t * TILE, TILE)
-        return remote(
-            moving[kind][source].at[:, rows],
-            moving[kind][target].at[:, rows],
-            zf_send.at[d, at],
-            zf_recv.at[d, at],
-            z_next[d],
-        )
-
-    def xg_copy(kind, d, n):
-        if n < 2:
-            src, dst = n * NH, (6 if d == 0 else 2) * NT + n * NH
-        else:
-            src = (6 if d == 0 else 2) * NT + d * NH
-            dst = 4 * NT + d * NH
-        return remote(
-            fixed[kind].at[pl.ds(src, NH)],
-            fixed[kind].at[pl.ds(dst, NH)],
-            xg_send.at[kind, d, n],
-            xg_recv.at[kind, d, n],
-            x_next[d],
-        )
-
-    def cg_copy(kind, dx):
-        return remote(
-            fixed[kind].at[pl.ds(2 * dx * NT, NT)],
-            fixed[kind].at[pl.ds((2 * dx + 1) * NT, NT)],
-            cg_send.at[kind, dx],
-            cg_recv.at[kind, dx],
-            other_core,
-        )
-
-    y_start(0)
-    for t in range(2):
-        for d in range(2):
-            zf_copy(d, 1, 0, t).start()
-            xg_copy(0, d, t).start()
     for o in range(1, NZ):
         req_copy(o).start()
-    cg_copy(0, 0).start()
 
     total = y_total(0)
     q_scale, k_scale = as_columns(lax.rsqrt(total / width_all + EPS))
@@ -565,43 +565,53 @@
             lax.fori_loop(0, NH, one, 0)
             zb_copy(d, level, t).start()
 
-    def rest_terms(r):
-        def one(i, carry):
-            for half in range(2):
-                place = 2 * i + half
-                term(r, place + jnp.where(i >= 2, 2, 0))
-            return carry
-
-        lax.fori_loop(0, NP // 2 - 1, one, 0)
-
     def opposite_terms(r):
         term(r, 4)
         term(r, 5)
 
+    def own_terms(r):
+        term(r, 0)
+        term(r, 1)
+
+    def side_terms(r):
+        def one(i, carry):
+            for half in range(2):
+                term(r, 4 * i + 2 + half)
+            return carry
+
+        lax.fori_loop(0, 2, one, 0)
+
     opposite_terms(4)
-    rest_terms(4)
+    own_terms(4)
+    side_terms(4)
     z_pass(0, 4)
     z_pass(1, 4)
     for r in (5, 3, 6, 2, 7, 1, 0):
         opposite_terms(r)
     to_core(2)
-    rest_terms(5)
+    own_terms(5)
+    side_terms(5)
     z_pass(1, 3)
-    rest_terms(3)
+    own_terms(3)
+    side_terms(3)
     z_pass(0, 3)
     cb_copy(2).wait_recv()
     x_pass(2, 0, 0)
     x_pass(2, 1, 1)
     for r in (6, 2, 7, 1, 0):
-        rest_terms(r)
+        side_terms(r)
     to_core(1)
     to_core(3)
-    z_pass(1, 2)
-    z_pass(0, 2)
+    for r in (6, 2):
+        own_terms(r)
     cb_copy(1).wait_recv()
     x_pass(1, 0, 1)
     cb_copy(3).wait_recv()
     x_pass(1, 1, 0)
+    z_pass(1, 2)
+    z_pass(0, 2)
+    for r in (7, 1, 0):
+        own_terms(r)
     x_pass(1, 0, 0)
     x_pass(1, 1, 1)
     to_core(0)
@@ -701,14 +711,20 @@
                     xb_copy(2, d, kind, t).wait_send()
 
 
-def place_results(a, b, c, a_out, b_out, c_out, sems):
-    copies = [
-        pltpu.make_async_copy(src, dst, sems.at[i])
-        for i, (src, dst) in enumerate(((a, a_out), (b, b_out), (c, c_out)))
+def place_results(a, b, c, a_out, b_out, c_out, held, sems):
+    coming = [
+        pltpu.make_async_copy(src, held.at[i], sems.at[0, i]) for i, src in enumerate((a, b, c))
     ]
-    for copy in copies:
+    going = [
+        pltpu.make_async_copy(held.at[i], dst, sems.at[1, i])
+        for i, dst in enumerate((a_out, b_out, c_out))
+    ]
+    for copy in coming:
         copy.start()
-    for copy in copies:
+    for came, goes in zip(coming, going):
+        came.wait()
+        goes.start()
+    for copy in going:
         copy.wait()
 
 
@@ -790,7 +806,7 @@
         out_shape=(out, out, out),
         in_specs=[anywhere] * 3,
         out_specs=(anywhere,) * 3,
-        scratch_shapes=[dma((3,))],
+        scratch_shapes=[pltpu.VMEM((3,) + q_pre.shape, BF16), dma((2, 3))],
         name="place_results",
     )(*results)
 

time: 149 us -> 123 us (0.83)
  Pallas kernels: 148 us -> 122 us
    pallas_call x1, Pallas kernels: 30.9 us -> 1.96 us  [on_device(): pl.pallas_call(place_results, out_shape=(out, out, out), in_specs=[anywhe...]
    pallas_call x1, Pallas kernels: 117 us -> 120 us  [on_device(): pl.pallas_call(functools.partial(kernel, width_all), out_shape=(out, out,...]
where the time goes in v4:
time: 123 us; the launch traced here: 122 us
  Pallas kernels  122 us (99%)
    pallas_call x1, Pallas kernels, on_device(): pl.pallas_call(functools.partial(kernel, width_all), out_shape=(out, out,...  120 us

profile of v4, /device:TPU:1, one launch (start us, length us, event | category | flops | bytes accessed | tf_op | source)
XLA Modules:
  0.0 122.5 jit_solution(9682965731116017236)
XLA Ops:
  0.6 119.9 %sparse_attention_backward.1 = (bf16[256,640]{1,0:T(8,128)(2,1)}, bf16[256,640]{1,0:T(8,128)(2,1)}, bf16[256,640]{1,0:T(8,128)(2,1)}) custom-call(s32[5,2,7]{2,1,0:T(2,128)} %bitcast.1, bf16[256,640]{1,0:T(8,128)(2,1)} %refs_1_.1, bf16[256,640]{1,0:T(8,128)(2,1)} %refs_2_.1, bf16[256,640]{1,0:T(8,128)(2,1)} %refs_3_.1, bf16[256,640]{1,0:T(8,128)(2,1)} %refs_4_.1, ...), custom_call_target="tpu_custom_call" | custom-call | tf_op jit(solution)/shard_map/sparse_attention_backward/pallas_call | solution.py:790
  120.5 2.0 %place_results.1 = (bf16[256,640]{1,0:T(8,128)(2,1)}, bf16[256,640]{1,0:T(8,128)(2,1)}, bf16[256,640]{1,0:T(8,128)(2,1)}) custom-call(bf16[256,640]{1,0:T(8,128)(2,1)} %get-tuple-element.6.a, bf16[256,640]{1,0:T(8,128)(2,1)} %get-tuple-element.7.b, bf16[256,640]{1,0:T(8,128)(2,1)} %get-tuple-element.8.c), custom_call_target="tpu_custom_call" | custom-call | tf_op jit(solution)/shard_map/place_results/pallas_call | solution.py:804

commit v5 on v3

--- a/solution.py
+++ b/solution.py
@@ -224,10 +224,12 @@
             other_core,
         )
 
+    for t in range(2):
+        for d in range(2):
+            zf_copy(d, 1, 0, t).start()
     y_start(0)
     for t in range(2):
         for d in range(2):
-            zf_copy(d, 1, 0, t).start()
             xg_copy(0, d, t).start()
     for o in range(1, NZ):
         req_copy(o).start()
@@ -378,29 +380,6 @@
     forward(3, 0)
     scores(6)
     scores(2)
-    forward(3, 1)
-    scores(5)
-    forward(4, 0)
-    scores(3)
-    gradient_scores(4)
-    forward(4, 1)
-    scores(4, with_dp=False)
-
-    for o in range(1, NZ):
-        req_copy(o).wait_send()
-    for hop in range(1, 5):
-        for kind in range(2):
-            for t in range(2):
-                for d in range(2):
-                    if hop < 4 or t == d:
-                        zf_copy(d, hop, kind, t).wait_send()
-    for kind in range(2):
-        for d in range(2):
-            for n in range(3):
-                xg_copy(kind, d, n).wait_send()
-        for dx in range(NX):
-            cg_copy(kind, dx).wait_send()
-
     row_at = lax.broadcasted_iota(jnp.int32, (NZ * NP, TOK), 0)
     head_at = jnp.full((NZ * NP, TOK), -1, jnp.int32)
     for h in range(NH):
@@ -410,6 +389,14 @@
             dx = ((owner & (NP - 1)) // 2 - x + NX) & (NX - 1)
             place = dx * 2 + ((owner + core) & 1)
             head_at = jnp.where(row_at == dz * NP + place, h, head_at)
+    forward(3, 1)
+    scores(5)
+    forward(4, 0)
+    scores(3)
+    gradient_scores(4)
+    forward(4, 1)
+    scores(4, with_dp=False)
+
     for r in range(1, NZ):
         st_copy(r).wait_recv()
     pair_lse = jnp.concatenate([stat_in[r, 0] for r in range(NZ)], axis=0)
@@ -435,6 +422,22 @@
     for o in (4, 3, 5, 2, 6, 1, 7):
         rp_copy(o).start()
     reply_in[0] = reply_out[...]
+
+    for o in range(1, NZ):
+        req_copy(o).wait_send()
+    for hop in range(1, 5):
+        for kind in range(2):
+            for t in range(2):
+                for d in range(2):
+                    if hop < 4 or t == d:
+                        zf_copy(d, hop, kind, t).wait_send()
+    for kind in range(2):
+        for d in range(2):
+            for n in range(3):
+                xg_copy(kind, d, n).wait_send()
+        for dx in range(NX):
+            cg_copy(kind, dx).wait_send()
+
     for o in range(1, NZ):
         rp_copy(o).wait_recv()
     for r in range(NZ):
@@ -641,7 +644,8 @@
         dq = dq_wide[h] + back_z[0, 0, h].astype(F32) + back_z[1, 0, h].astype(F32)
         dq_wide[h] = dq
         dots += gain(q_gain, h) * dq * q_in[:, cols].astype(F32)
-    q_dot = jnp.sum(dots, axis=1, keepdims=True)
+    y_out[1] = as_rows(jnp.sum(dots, axis=1, keepdims=True), 0.0)
+    y_start(1)
 
     for t in range(2):
         for d in range(2):
@@ -654,26 +658,33 @@
         for h in range(NH):
             cols = slice(h * HD, (h + 1) * HD)
             b = t * NH + h
-            dv = dv_sum[b] + x_in[0, 0, b].astype(F32) + x_in[0, 1, b].astype(F32)
-            dv_out[rows, cols] = dv.astype(BF16)
             dk = dk_sum[b] + x_in[0, 0, NT + b].astype(F32) + x_in[0, 1, NT + b].astype(F32)
             dk_sum[b] = dk
             dots += gain(k_gain, h) * dk * k_in[rows, cols].astype(F32)
         columns.append(jnp.sum(dots, axis=1, keepdims=True))
-    y_out[1] = as_rows(q_dot, jnp.concatenate(columns, axis=0))
-    y_start(1)
+    y_out[2] = as_rows(jnp.concatenate(columns, axis=0), 0.0)
+    y_start(2)
 
     def finish(wide, gains, grad, scale, dot_mean):
         return (scale * gains * grad - wide * (scale * scale * scale) * dot_mean).astype(BF16)
 
-    q_dot, k_dot = as_columns(y_total(1) / width_all)
+    for t in range(2):
+        rows = slice(t * TILE, (t + 1) * TILE)
+        for h in range(NH):
+            b = t * NH + h
+            dv = dv_sum[b] + x_in[0, 0, b].astype(F32) + x_in[0, 1, b].astype(F32)
+            dv_out[rows, h * HD : (h + 1) * HD] = dv.astype(BF16)
+    q_dot, _ = as_columns(y_total(1) / width_all)
     for h in range(NH):
         cols = slice(h * HD, (h + 1) * HD)
         dq_out[:, cols] = finish(
             q_in[:, cols].astype(F32), gain(q_gain, h), dq_wide[h], q_scale_ref[...], q_dot
         )
-        for t in range(2):
-            rows = slice(t * TILE, (t + 1) * TILE)
+    k_dot, _ = as_columns(y_total(2) / width_all)
+    for t in range(2):
+        rows = slice(t * TILE, (t + 1) * TILE)
+        for h in range(NH):
+            cols = slice(h * HD, (h + 1) * HD)
             dk_out[rows, cols] = finish(
                 k_in[rows, cols].astype(F32),
                 gain(k_gain, h),
@@ -682,7 +693,7 @@
                 k_dot[rows],
             )
 
-    for n in range(2):
+    for n in range(3):
         for p in range(1, NY):
             y_copy(n, p).wait_send()
     for r in range(1, NZ):
@@ -701,14 +712,20 @@
                     xb_copy(2, d, kind, t).wait_send()
 
 
-def place_results(a, b, c, a_out, b_out, c_out, sems):
-    copies = [
-        pltpu.make_async_copy(src, dst, sems.at[i])
-        for i, (src, dst) in enumerate(((a, a_out), (b, b_out), (c, c_out)))
+def place_results(a, b, c, a_out, b_out, c_out, held, sems):
+    coming = [
+        pltpu.make_async_copy(src, held.at[i], sems.at[0, i]) for i, src in enumerate((a, b, c))
     ]
-    for copy in copies:
+    going = [
+        pltpu.make_async_copy(held.at[i], dst, sems.at[1, i])
+        for i, dst in enumerate((a_out, b_out, c_out))
+    ]
+    for copy in coming:
         copy.start()
-    for copy in copies:
+    for came, goes in zip(coming, going):
+        came.wait()
+        goes.start()
+    for copy in going:
         copy.wait()
 
 
@@ -744,8 +761,8 @@
         pltpu.VMEM((NT, TILE, HD), F32),
         pltpu.VMEM((TOK, 128), F32),
         pltpu.VMEM((TOK, 128), F32),
-        pltpu.VMEM((2, 8, TOK), F32),
-        pltpu.VMEM((2, NY - 1, 8, TOK), F32),
+        pltpu.VMEM((3, 8, TOK), F32),
+        pltpu.VMEM((3, NY - 1, 8, TOK), F32),
         pltpu.VMEM((NZ, 8, 128), jnp.int32),
         pltpu.SMEM((NZ, 8, 128), jnp.int32),
         dma((2, 16)),
@@ -764,8 +781,8 @@
         dma((NX,)),
         dma((2, 2, 2, 2)),
         dma((2, 2, 2, 2)),
-        dma((2, NY - 1)),
-        dma((2, NY - 1)),
+        dma((3, NY - 1)),
+        dma((3, NY - 1)),
         dma((NZ - 1,)),
         dma((NZ - 1,)),
         dma((1,)),
@@ -790,7 +807,7 @@
         out_shape=(out, out, out),
         in_specs=[anywhere] * 3,
         out_specs=(anywhere,) * 3,
-        scratch_shapes=[dma((3,))],
+        scratch_shapes=[pltpu.VMEM((3,) + q_pre.shape, BF16), dma((2, 3))],
         name="place_results",
     )(*results)
 

time: 149 us -> 120 us (0.81)
  Pallas kernels: 148 us -> 119 us
    pallas_call x1, Pallas kernels: 30.9 us -> 1.96 us  [on_device(): pl.pallas_call(place_results, out_shape=(out, out, out), in_specs=[anywhe...]
where the time goes in v5:
time: 120 us
  Pallas kernels  119 us (99%)
    pallas_call x1, Pallas kernels, on_device(): pl.pallas_call(functools.partial(kernel, width_all), out_shape=(out, out,...  117 us

profile of v5, /device:TPU:1, one launch (start us, length us, event | category | flops | bytes accessed | tf_op | source)
XLA Modules:
  0.0 119.7 jit_solution(17241148126954394664)
XLA Ops:
  0.6 117.1 %sparse_attention_backward.1 = (bf16[256,640]{1,0:T(8,128)(2,1)}, bf16[256,640]{1,0:T(8,128)(2,1)}, bf16[256,640]{1,0:T(8,128)(2,1)}) custom-call(s32[5,2,7]{2,1,0:T(2,128)} %bitcast.1, bf16[256,640]{1,0:T(8,128)(2,1)} %refs_1_.1, bf16[256,640]{1,0:T(8,128)(2,1)} %refs_2_.1, bf16[256,640]{1,0:T(8,128)(2,1)} %refs_3_.1, bf16[256,640]{1,0:T(8,128)(2,1)} %refs_4_.1, ...), custom_call_target="tpu_custom_call" | custom-call | tf_op jit(solution)/shard_map/sparse_attention_backward/pallas_call | solution.py:791
  117.7 2.0 %place_results.1 = (bf16[256,640]{1,0:T(8,128)(2,1)}, bf16[256,640]{1,0:T(8,128)(2,1)}, bf16[256,640]{1,0:T(8,128)(2,1)}) custom-call(bf16[256,640]{1,0:T(8,128)(2,1)} %get-tuple-element.6.a, bf16[256,640]{1,0:T(8,128)(2,1)} %get-tuple-element.7.b, bf16[256,640]{1,0:T(8,128)(2,1)} %get-tuple-element.8.c), custom_call_target="tpu_custom_call" | custom-call | tf_op jit(solution)/shard_map/place_results/pallas_call | solution.py:805

commit v6 on v5

--- a/solution.py
+++ b/solution.py
@@ -72,6 +72,7 @@
         lse_ref,
         delta_ref,
         dq_wide,
+        dq_rows,
         dk_sum,
         dv_sum,
         q_scale_ref,
@@ -455,7 +456,7 @@
         ds = (probs * (dp_all[pair] - delta_ref[r * NH + head][:1]) * FACTOR).astype(BF16)
         dv = dot_nn(probs.astype(BF16), g_bufs[r][head])
         dk = dot_nn(ds, q_bufs[r][head])
-        dq = dot_tn(ds, k_all[place * NT + code])
+        dq = dot_tn(k_all[place * NT + code], ds)
         kv_terms[2 * pair] = dv.astype(BF16)
         kv_terms[2 * pair + 1] = dk.astype(BF16)
         q_terms[pair] = dq.astype(BF16)
@@ -478,12 +479,12 @@
         )
 
     def query_sum(r, t, h):
-        rows = slice(t * TILE, (t + 1) * TILE)
+        cols = slice(t * TILE, (t + 1) * TILE)
         return tree(
             [
                 jnp.where(
                     lax.rem(jnp.maximum(code_of(r, place), 0), NH) == h,
-                    q_terms[r * NP + place, rows],
+                    q_terms[r * NP + place, :, cols],
                     zero_tile,
                 )
                 for place in range(NP)
@@ -607,25 +608,25 @@
     x_pass(1, 1, 0)
     x_pass(1, 0, 0)
     x_pass(1, 1, 1)
+    z_pass(1, 1)
+    z_pass(0, 1)
     to_core(0)
 
     def near_terms(h, carry):
-        dq = jnp.zeros((TOK, HD), F32)
+        dq = jnp.zeros((HD, TOK), F32)
         lse, delta = lse_ref[h][:1], delta_ref[h][:1]
         for t in range(2):
             probs = jnp.exp(s_near[h, t] - lse)
             ds = (probs * (dp_near[h, t] - delta) * FACTOR).astype(BF16)
             dv_sum[t * NH + h] = dot_nn(probs.astype(BF16), g_bufs[0][h])
             dk_sum[t * NH + h] = dot_nn(ds, q_bufs[0][h])
-            dq += dot_tn(ds, k_all[t * NH + h])
+            dq += dot_tn(k_all[t * NH + h], ds)
         dq_wide[h] = dq
         for t in range(2):
-            dq_wide[h, t * TILE : (t + 1) * TILE] += query_sum(0, t, h)
+            dq_wide[h, :, t * TILE : (t + 1) * TILE] += query_sum(0, t, h)
         return carry
 
     lax.fori_loop(0, NH, near_terms, 0)
-    z_pass(1, 1)
-    z_pass(0, 1)
     cb_copy(0).wait_recv()
 
     def own_sum(block, carry):
@@ -641,9 +642,11 @@
     dots = jnp.zeros((TOK, HD), F32)
     for h in range(NH):
         cols = slice(h * HD, (h + 1) * HD)
-        dq = dq_wide[h] + back_z[0, 0, h].astype(F32) + back_z[1, 0, h].astype(F32)
-        dq_wide[h] = dq
-        dots += gain(q_gain, h) * dq * q_in[:, cols].astype(F32)
+        for t in range(2):
+            rows = slice(t * TILE, (t + 1) * TILE)
+            came = back_z[0, 0, h, rows].astype(F32) + back_z[1, 0, h, rows].astype(F32)
+            dq_rows[h, rows] = jnp.transpose(dq_wide[h, :, rows] + came)
+        dots += gain(q_gain, h) * dq_rows[h] * q_in[:, cols].astype(F32)
     y_out[1] = as_rows(jnp.sum(dots, axis=1, keepdims=True), 0.0)
     y_start(1)
 
@@ -678,7 +681,7 @@
     for h in range(NH):
         cols = slice(h * HD, (h + 1) * HD)
         dq_out[:, cols] = finish(
-            q_in[:, cols].astype(F32), gain(q_gain, h), dq_wide[h], q_scale_ref[...], q_dot
+            q_in[:, cols].astype(F32), gain(q_gain, h), dq_rows[h], q_scale_ref[...], q_dot
         )
     k_dot, _ = as_columns(y_total(2) / width_all)
     for t in range(2):
@@ -741,7 +744,7 @@
         pltpu.VMEM((pairs, TILE, TOK), F32),
         pltpu.VMEM((pairs, TILE, TOK), F32),
         pltpu.VMEM((2 * pairs, TILE, HD), BF16),
-        pltpu.VMEM((pairs, TOK, HD), BF16),
+        pltpu.VMEM((pairs, HD, TOK), BF16),
         pltpu.VMEM((2, 4, NH, TOK, HD), BF16),
         pltpu.VMEM((NX * 2 * NT, TILE, HD), BF16),
         pltpu.VMEM((NX * 2 * NT, TILE, HD), BF16),
@@ -756,6 +759,7 @@
         pltpu.VMEM((NZ, 16, TOK), F32),
         pltpu.VMEM((NZ * NH, 8, TOK), F32),
         pltpu.VMEM((NZ * NH, 8, TOK), F32),
+        pltpu.VMEM((NH, HD, TOK), F32),
         pltpu.VMEM((NH, TOK, HD), F32),
         pltpu.VMEM((NT, TILE, HD), F32),
         pltpu.VMEM((NT, TILE, HD), F32),

time: 120 us -> 120 us (level)
  no operation moved by 1% of the time
where the time goes in v6:
time: 120 us
  Pallas kernels  119 us (99%)
    pallas_call x1, Pallas kernels, on_device(): pl.pallas_call(functools.partial(kernel, width_all), out_shape=(out, out,...  117 us

profile of v6, /device:TPU:1, one launch (start us, length us, event | category | flops | bytes accessed | tf_op | source)
XLA Modules:
  0.0 119.8 jit_solution(4382616832685341526)
XLA Ops:
  0.6 117.2 %sparse_attention_backward.1 = (bf16[256,640]{1,0:T(8,128)(2,1)}, bf16[256,640]{1,0:T(8,128)(2,1)}, bf16[256,640]{1,0:T(8,128)(2,1)}) custom-call(s32[5,2,7]{2,1,0:T(2,128)} %bitcast.1, bf16[256,640]{1,0:T(8,128)(2,1)} %refs_1_.1, bf16[256,640]{1,0:T(8,128)(2,1)} %refs_2_.1, bf16[256,640]{1,0:T(8,128)(2,1)} %refs_3_.1, bf16[256,640]{1,0:T(8,128)(2,1)} %refs_4_.1, ...), custom_call_target="tpu_custom_call" | custom-call | tf_op jit(solution)/shard_map/sparse_attention_backward/pallas_call | solution.py:795
  117.8 2.0 %place_results.1 = (bf16[256,640]{1,0:T(8,128)(2,1)}, bf16[256,640]{1,0:T(8,128)(2,1)}, bf16[256,640]{1,0:T(8,128)(2,1)}) custom-call(bf16[256,640]{1,0:T(8,128)(2,1)} %get-tuple-element.6.a, bf16[256,640]{1,0:T(8,128)(2,1)} %get-tuple-element.7.b, bf16[256,640]{1,0:T(8,128)(2,1)} %get-tuple-element.8.c), custom_call_target="tpu_custom_call" | custom-call | tf_op jit(solution)/shard_map/place_results/pallas_call | solution.py:809

commit v7 on v5

--- a/solution.py
+++ b/solution.py
@@ -21,6 +21,7 @@
 EPS = 1e-6
 FACTOR = 1.0 / math.sqrt(HD)
 MESH = pl.DeviceIdType.MESH
+Z_ORDER = ((0, 0), (1, 1), (0, 1), (1, 0))
 F32 = jnp.float32
 BF16 = jnp.bfloat16
 
@@ -224,9 +225,8 @@
             other_core,
         )
 
-    for t in range(2):
-        for d in range(2):
-            zf_copy(d, 1, 0, t).start()
+    for d, t in Z_ORDER:
+        zf_copy(d, 1, 0, t).start()
     y_start(0)
     for t in range(2):
         for d in range(2):
@@ -254,8 +254,11 @@
                 k_in[rows, cols].astype(F32) * k_scale_ref[rows] * gain(k_gain, h)
             ).astype(BF16)
         for d in range(2):
-            zf_copy(d, 1, 1, t).start()
             xg_copy(1, d, t).start()
+            if t == 1:
+                zf_copy(d, 1, 1, d).start()
+    for d in range(2):
+        zf_copy(d, 1, 1, 1 - d).start()
     cg_copy(1, 0).start()
 
     for o in range(1, NZ):
@@ -341,12 +344,11 @@
             st_copy(r).start()
 
     def forward(hop, kind):
-        for t in range(2):
-            for d in range(2):
-                if hop < 4 or t == d:
-                    zf_copy(d, hop, kind, t).wait_recv()
-                if hop < 3 or (hop == 3 and t == d):
-                    zf_copy(d, hop + 1, kind, t).start()
+        for d, t in Z_ORDER:
+            if hop < 4 or t == d:
+                zf_copy(d, hop, kind, t).wait_recv()
+            if hop < 3 or (hop == 3 and t == d):
+                zf_copy(d, hop + 1, kind, t).start()
 
     def plane_first(kind):
         for t in range(2):
@@ -379,7 +381,6 @@
     scores(1)
     forward(3, 0)
     scores(6)
-    scores(2)
     row_at = lax.broadcasted_iota(jnp.int32, (NZ * NP, TOK), 0)
     head_at = jnp.full((NZ * NP, TOK), -1, jnp.int32)
     for h in range(NH):
@@ -390,6 +391,7 @@
             place = dx * 2 + ((owner + core) & 1)
             head_at = jnp.where(row_at == dz * NP + place, h, head_at)
     forward(3, 1)
+    scores(2)
     scores(5)
     forward(4, 0)
     scores(3)
@@ -552,7 +554,7 @@
 
     def z_pass(d, level):
         r = level if d == 0 else NZ - level
-        for t in (1 - d, d) if level == 3 else ((d,) if level == 4 else (0, 1)):
+        for t in (d,) if level == 4 else (1 - d, d):
             chained = level < 3 or (level == 3 and t == d)
             rows = slice(t * TILE, (t + 1) * TILE)
             if chained:

time: 120 us -> 120 us (level)
  no operation moved by 1% of the time
where the time goes in v7:
time: 120 us
  Pallas kernels  119 us (99%)
    pallas_call x1, Pallas kernels, on_device(): pl.pallas_call(functools.partial(kernel, width_all), out_shape=(out, out,...  117 us

profile of v7, /device:TPU:1, one launch (start us, length us, event | category | flops | bytes accessed | tf_op | source)
XLA Modules:
  0.0 119.7 jit_solution(3185164904185663358)
XLA Ops:
  0.6 117.1 %sparse_attention_backward.1 = (bf16[256,640]{1,0:T(8,128)(2,1)}, bf16[256,640]{1,0:T(8,128)(2,1)}, bf16[256,640]{1,0:T(8,128)(2,1)}) custom-call(s32[5,2,7]{2,1,0:T(2,128)} %bitcast.1, bf16[256,640]{1,0:T(8,128)(2,1)} %refs_1_.1, bf16[256,640]{1,0:T(8,128)(2,1)} %refs_2_.1, bf16[256,640]{1,0:T(8,128)(2,1)} %refs_3_.1, bf16[256,640]{1,0:T(8,128)(2,1)} %refs_4_.1, ...), custom_call_target="tpu_custom_call" | custom-call | tf_op jit(solution)/shard_map/sparse_attention_backward/pallas_call | solution.py:793
  117.8 2.0 %place_results.1 = (bf16[256,640]{1,0:T(8,128)(2,1)}, bf16[256,640]{1,0:T(8,128)(2,1)}, bf16[256,640]{1,0:T(8,128)(2,1)}) custom-call(bf16[256,640]{1,0:T(8,128)(2,1)} %get-tuple-element.6.a, bf16[256,640]{1,0:T(8,128)(2,1)} %get-tuple-element.7.b, bf16[256,640]{1,0:T(8,128)(2,1)} %get-tuple-element.8.c), custom_call_target="tpu_custom_call" | custom-call | tf_op jit(solution)/shard_map/place_results/pallas_call | solution.py:807

commit v8 on v5

--- a/solution.py
+++ b/solution.py
@@ -45,7 +45,7 @@
 
 
 def kernel(width_all, *refs):
-    sel, q_in, k_in, v_in, g_in, q_gain, k_gain, dq_out, dk_out, dv_out = refs[:10]
+    sel, q_hbm, k_hbm, v_hbm, g_in, q_gain, k_gain, dq_out, dk_out, dv_out = refs[:10]
     scratch = list(refs[10:])
     g_bufs = [scratch.pop(0) for _ in range(NZ)]
     q_bufs = [scratch.pop(0) for _ in range(NZ)]
@@ -101,7 +101,17 @@
         rq_send,
         rq_recv,
         here_sem,
+        q_in,
+        k_in,
+        v_in,
+        in_sem,
     ) = scratch
+    loads = [
+        pltpu.make_async_copy(src, dst, in_sem.at[i])
+        for i, (src, dst) in enumerate(((q_hbm, q_in), (k_hbm, k_in), (v_hbm, v_in)))
+    ]
+    for load in loads:
+        load.start()
     fixed = (v_all, k_all)
 
     me = lax.axis_index("ctx")
@@ -142,8 +152,6 @@
     for h in range(NH):
         cols = slice(h * HD, (h + 1) * HD)
         g_bufs[0][h] = g_in[:, cols]
-        for t in range(2):
-            v_all[t * NH + h] = v_in[t * TILE : (t + 1) * TILE, cols]
     lane = lax.broadcasted_iota(jnp.int32, (8, 128), 1)
     wanted = jnp.full((8, 128), -1, jnp.int32)
     for h in range(NH):
@@ -180,7 +188,6 @@
             y_copy(n, p).wait_recv()
         return (y_out[n] + y_in[n, 0]) + (y_in[n, 1] + y_in[n, 2])
 
-    y_out[0] = as_rows(squares(q_in), squares(k_in))
     pl.semaphore_wait(barrier, len(peers))
 
     def req_copy(o):
@@ -227,7 +234,13 @@
     for t in range(2):
         for d in range(2):
             zf_copy(d, 1, 0, t).start()
+    for load in loads:
+        load.wait()
+    y_out[0] = as_rows(squares(q_in), squares(k_in))
     y_start(0)
+    for h in range(NH):
+        for t in range(2):
+            v_all[t * NH + h] = v_in[t * TILE : (t + 1) * TILE, h * HD : (h + 1) * HD]
     for t in range(2):
         for d in range(2):
             xg_copy(0, d, t).start()
@@ -786,12 +799,18 @@
         dma((NZ - 1,)),
         dma((NZ - 1,)),
         dma((1,)),
+        pltpu.VMEM(q_pre.shape, BF16),
+        pltpu.VMEM(q_pre.shape, BF16),
+        pltpu.VMEM(q_pre.shape, BF16),
+        dma((3,)),
     ]
     out = jax.ShapeDtypeStruct(q_pre.shape, BF16)
     results = pl.pallas_call(
         functools.partial(kernel, width_all),
         out_shape=(out, out, out),
-        in_specs=[pl.BlockSpec(memory_space=pltpu.SMEM)] + [vmem] * 6,
+        in_specs=[pl.BlockSpec(memory_space=pltpu.SMEM)]
+        + [pl.BlockSpec(memory_space=pl.ANY)] * 3
+        + [vmem] * 3,
         out_specs=(vmem, vmem, vmem),
         scratch_shapes=scratch,
         compiler_params=pltpu.CompilerParams(

time: 120 us -> 120 us (level)
  no operation moved by 1% of the time
where the time goes in v8:
time: 120 us; the launch traced here: 119 us
  Pallas kernels  119 us (99%)
    pallas_call x1, Pallas kernels, on_device(): pl.pallas_call(functools.partial(kernel, width_all), out_shape=(out, out,...  117 us

profile of v8, /device:TPU:1, one launch (start us, length us, event | category | flops | bytes accessed | tf_op | source)
XLA Modules:
  0.0 119.4 jit_solution(15624974521750564128)
XLA Ops:
  0.6 116.8 %sparse_attention_backward.1 = (bf16[256,640]{1,0:T(8,128)(2,1)}, bf16[256,640]{1,0:T(8,128)(2,1)}, bf16[256,640]{1,0:T(8,128)(2,1)}) custom-call(s32[5,2,7]{2,1,0:T(2,128)} %bitcast.1, bf16[256,640]{1,0:T(8,128)(2,1)} %refs_1_.1, bf16[256,640]{1,0:T(8,128)(2,1)} %refs_2_.1, bf16[256,640]{1,0:T(8,128)(2,1)} %refs_3_.1, bf16[256,640]{1,0:T(8,128)(2,1)} %refs_4_.1, ...), custom_call_target="tpu_custom_call" | custom-call | tf_op jit(solution)/shard_map/sparse_attention_backward/pallas_call | solution.py:808
  117.4 2.0 %place_results.1 = (bf16[256,640]{1,0:T(8,128)(2,1)}, bf16[256,640]{1,0:T(8,128)(2,1)}, bf16[256,640]{1,0:T(8,128)(2,1)}) custom-call(bf16[256,640]{1,0:T(8,128)(2,1)} %get-tuple-element.6.a, bf16[256,640]{1,0:T(8,128)(2,1)} %get-tuple-element.7.b, bf16[256,640]{1,0:T(8,128)(2,1)} %get-tuple-element.8.c), custom_call_target="tpu_custom_call" | custom-call | tf_op jit(solution)/shard_map/place_results/pallas_call | solution.py:824
